TPU v7x, 128 devices: a whole 4x4x4 slice. The times are simulated.
128 devices in a mesh: win: 4 (over x_hi, core), chan: 32 (over y, x_lo, z).
Axes of the slice: x: 4 (x_hi: 2, x_lo: 2; x = x_hi * 2 + x_lo), y: 4, z: 4, core: 2. Of those that a mesh axis runs over, the one named last changes fastest.
Arguments:
- source_spectra: bfloat16 [32, 4096, 1024], P('win', 'chan'), may hold values from -6 to 6
- receiver_spectra: bfloat16 [32, 128, 1024], P('win', 'chan'), may hold values from -6 to 6
- quality_mask: int32 [32, 128], P('win', 'chan'), may hold values 0 or 1
- owner_plan: int32 [6], replicated, may hold values from 0 to 31
Outputs:
- correlations: bfloat16 [6, 128, 128, 4096], P(None, None, 'chan', 'win')
All inputs are finite; a program needn't handle non-finite values. No bound on the sum of `quality_mask` on one device may be relied on, other than what follows from the above.
Results may differ from a plain program's by a relative error of at most 0.0055.
Values may be sent and summed in bfloat16 or wider, within the bound.
No kernel may reach another device: no remote copies, remote signals or barrier semaphores. Data moves between devices by JAX's collectives and lax.ppermute only.
A program may use at most 128 MiB of HBM per device.

v0:
```python
import math

import jax
import jax.numpy as jnp
from jax import lax
from jax.sharding import PartitionSpec as P

LAGS = 4096
STEPS = 6


def spread(block, axis, owner):
    block = jnp.where(lax.axis_index(axis) == owner, block, jnp.zeros_like(block))
    return lax.psum(block, axis)


def build_table(start, count, bin_count, lag_count, scale):
    rows = jnp.arange(2 * bin_count, dtype=jnp.int32)
    wave = rows % bin_count + bin_count // 8
    shift = jnp.arange(count, dtype=jnp.int32) + start - lag_count // 2
    phase = wave[:, None] * shift[None, :] % (2 * lag_count)
    angle = phase.astype(jnp.float32) * (math.pi / lag_count)
    table = jnp.where(rows[:, None] < bin_count, jnp.cos(angle), -jnp.sin(angle)) * scale
    return table.astype(jnp.bfloat16)


def build_taper(start, count, lag_count):
    position = jnp.arange(count, dtype=jnp.int32) + start
    edge = jnp.minimum(position, lag_count - 1 - position) + 1
    return jnp.minimum(1.0, edge.astype(jnp.float32) / (lag_count // 16))


def cross_spectra(source_block, rec_real, rec_imag):
    bin_count = rec_real.shape[2]
    src_real = source_block[:, :, :bin_count]
    src_imag = source_block[:, :, bin_count:]

    def contract(left, right):
        return jnp.einsum("wkf,wrf->krf", left, right, preferred_element_type=jnp.float32)

    real_part = contract(src_real, rec_real) + contract(src_imag, rec_imag)
    imag_part = contract(src_imag, rec_real) - contract(src_real, rec_imag)
    return jnp.concatenate([real_part, imag_part], axis=2)


def project(stack_rounded, lag_table, lag_taper):
    sources, receivers, width = stack_rounded.shape
    flat = jnp.dot(
        stack_rounded.reshape(sources * receivers, width),
        lag_table,
        preferred_element_type=jnp.float32,
    )
    return (flat.reshape(sources, receivers, lag_table.shape[1]) * lag_taper).astype(jnp.bfloat16)


def shards(source_spectra, receiver_spectra, quality_mask, owner_plan):
    win_groups = lax.axis_size("win")
    bin_count = receiver_spectra.shape[2] // 2
    lag_count = LAGS
    scale = 1.0 / math.sqrt(bin_count * source_spectra.shape[0] * win_groups)
    masked = receiver_spectra * quality_mask.astype(jnp.bfloat16)[:, :, None]
    rec_real = masked[:, :, :bin_count]
    rec_imag = masked[:, :, bin_count:]
    quarter = lag_count // win_groups
    first_lag = lax.axis_index("win") * quarter
    lag_table = build_table(first_lag, quarter, bin_count, lag_count, scale)
    lag_taper = build_taper(first_lag, quarter, lag_count)
    results = []
    for sweep_index in range(STEPS):
        owner_index = owner_plan[sweep_index]
        source_block = spread(source_spectra, "chan", owner_index)
        cross_stack = cross_spectra(source_block, rec_real, rec_imag)
        summed = lax.psum(cross_stack, "win")
        correlated = project(summed.astype(jnp.bfloat16), lag_table, lag_taper)
        results.append(correlated)
    return jnp.stack(results)


def solution(mesh):
    return jax.shard_map(
        shards,
        mesh=mesh,
        in_specs=(P("win", "chan", None), P("win", "chan", None), P("win", "chan"), P()),
        out_specs=P(None, None, "chan", "win"),
        check_vma=False,
    )
```

profile of v0, /device:TPU:1, one launch (start us, length us, event | category | flops | bytes accessed | tf_op | source)
XLA Modules:
  0.0 869.8 jit_solution(13623168343159424665)
XLA Ops:
  11.8 5.9 broadcast_select_fusion
  19.4 349.1 %all-reduce.5.cloned.1.call-done = (bf16[8,128,1024]{2,1,0:T(8,128)(2,1)}, bf16[8,128,1024]{2,1,0:T(8,128)(2,1)}, bf16[8,128,1024]{2,1,0:T(8,128)(2,1)}, bf16[8,...) async-done(((bf16[8,128,1024]{2,1,0:T(8,128)(2,1)}, bf16[8,128,1024]{2,1,0:T(8,128)(2,1)}, bf16[8,128,1024]{2,1,0:T(8,128)(2,1)}, ...) | async-done | bytes 12582928 | tf_op jit(solution)/shard_map/psum | solution.py:14
  368.4 3.9 fusion.127
  381.5 1.8 copy.35
  390.8 1.8 fusion.129
  402.8 2.2 copy.23
  412.6 1.8 fusion.131
  428.7 2.0 copy.11
  437.5 2.5 copy.44
  443.4 2.5 copy.36
  445.9 2.5 copy.37
  448.5 2.6 copy.38
  457.3 2.6 copy.30
  459.8 2.5 copy.31
  462.4 2.6 copy.32
  471.1 2.6 copy.24
  473.7 2.5 copy.25
  476.2 2.6 copy.26
  485.1 2.5 copy.18
  487.7 2.6 copy.19
  490.3 2.6 copy.20
  499.1 2.5 copy.9
  501.6 2.5 copy.14
  504.2 2.6 copy.13
  511.4 234.0 %all-reduce.6 = (bf16[128,4,1024]{2,0,1:T(8,128)(2,1)}, bf16[128,4,1024]{2,0,1:T(8,128)(2,1)}, bf16[128,4,1024]{2,0,1:T(8,128)(2,1)}, bf16[128,4,1024]{2,0,1:T(8...) all-reduce(f32[128,4,1024]{2,0,1:T(8,128)} %pad_maximum_fusion, ...), channel_id=1, replica_groups=mesh['win'=4,'chan'=32] {'win'}, use_global_device_ids=true, to_apply=%region_1.2 | all-reduce | flops 3145728 | bytes 18874368 | tf_op jit(solution)/shard_map/psum | solution.py:73
  745.4 19.1 %fusion.49 = bf16[6,128,4,1024]{3,1,2,0:T(8,128)(2,1)S(1)} fusion(s32[1024]{0:T(1024)S(1)} %get-tuple-element.50, s32[1024]{0:T(1024)S(1)} %get-tuple-element.49, pred[1024]{0:T(1024)(128)(4,1)S(1)} %iota_compare_fusion, f32[1024]{0:T(1024)S(1)} %fusion.92, bf16[128,4,1024]{2,0,1:T(8,128)(2,1)} %get-tuple-element.5), kind=kOutput, calls=%fused_computation.53 | convolution fusion | flops 1093664768 | bytes 2110464 | tf_op jit(solution)/shard_map/dot_general | solution.py:48
  764.5 18.3 %fusion.55 = bf16[6,128,4,1024]{3,1,2,0:T(8,128)(2,1)S(1)} fusion(bf16[6,128,4,1024]{3,1,2,0:T(8,128)(2,1)S(1)} %fusion.49, s32[1024]{0:T(1024)S(1)} %get-tuple-element.50, s32[1024]{0:T(1024)S(1)} %get-tuple-element.49, pred[1024]{0:T(1024)(128)(4,1)S(1)} %iota_compare_fusion, bf16[128,4,1024]{2,0,1:T(8,128)(2,1)S(1)} %copy-done.12, f32[1024]{0:T(1024)S(1)} %fusion.92), kind=kOutput, calls=%fused_computation.55 | convolution fusion | flops 1093664768 | bytes 2110464 | tf_op jit(solution)/shard_map/dot_general | solution.py:48
  782.8 17.9 %fusion.61 = bf16[6,128,4,1024]{3,1,2,0:T(8,128)(2,1)S(1)} fusion(bf16[6,128,4,1024]{3,1,2,0:T(8,128)(2,1)S(1)} %fusion.55, s32[1024]{0:T(1024)S(1)} %get-tuple-element.50, s32[1024]{0:T(1024)S(1)} %get-tuple-element.49, pred[1024]{0:T(1024)(128)(4,1)S(1)} %iota_compare_fusion, bf16[128,4,1024]{2,0,1:T(8,128)(2,1)S(1)} %copy-done.11, f32[1024]{0:T(1024)S(1)} %fusion.92), kind=kOutput, calls=%fused_computation.57 | convolution fusion | flops 1093664768 | bytes 2110464 | tf_op jit(solution)/shard_map/dot_general | solution.py:48
  800.7 18.3 %fusion.67 = bf16[6,128,4,1024]{3,1,2,0:T(8,128)(2,1)S(1)} fusion(bf16[6,128,4,1024]{3,1,2,0:T(8,128)(2,1)S(1)} %fusion.61, s32[1024]{0:T(1024)S(1)} %get-tuple-element.50, s32[1024]{0:T(1024)S(1)} %get-tuple-element.49, pred[1024]{0:T(1024)(128)(4,1)S(1)} %iota_compare_fusion, bf16[128,4,1024]{2,0,1:T(8,128)(2,1)S(1)} %copy-done.10, f32[1024]{0:T(1024)S(1)} %fusion.92), kind=kOutput, calls=%fused_computation.59 | convolution fusion | flops 1093664768 | bytes 2110464 | tf_op jit(solution)/shard_map/dot_general | solution.py:48
  819.0 17.8 %fusion.73 = bf16[6,128,4,1024]{3,1,2,0:T(8,128)(2,1)S(1)} fusion(bf16[6,128,4,1024]{3,1,2,0:T(8,128)(2,1)S(1)} %fusion.67, s32[1024]{0:T(1024)S(1)} %get-tuple-element.50, s32[1024]{0:T(1024)S(1)} %get-tuple-element.49, pred[1024]{0:T(1024)(128)(4,1)S(1)} %iota_compare_fusion, bf16[128,4,1024]{2,0,1:T(8,128)(2,1)S(1)} %copy-done.9, f32[1024]{0:T(1024)S(1)} %fusion.92), kind=kOutput, calls=%fused_computation.61 | convolution fusion | flops 1093664768 | bytes 2110464 | tf_op jit(solution)/shard_map/dot_general | solution.py:48
  836.8 18.1 %fusion.79 = bf16[6,128,4,1024]{3,1,2,0:T(8,128)(2,1)S(1)} fusion(bf16[6,128,4,1024]{3,1,2,0:T(8,128)(2,1)S(1)} %fusion.73, s32[1024]{0:T(1024)S(1)} %get-tuple-element.50, s32[1024]{0:T(1024)S(1)} %get-tuple-element.49, pred[1024]{0:T(1024)(128)(4,1)S(1)} %iota_compare_fusion, bf16[128,4,1024]{2,0,1:T(8,128)(2,1)S(1)} %copy-done.8, f32[1024]{0:T(1024)S(1)} %fusion.92), kind=kOutput, calls=%fused_computation.63 | convolution fusion | flops 1093664768 | bytes 2110464 | tf_op jit(solution)/shard_map/dot_general | solution.py:48
  854.9 7.6 copy.6
  (97 shorter events, 91.5 us)
Async XLA Ops:
  6.5 361.9 %all-reduce.5.cloned.1.call-start = ((), (), s32[]{:S(2)}) async-start(), calls=%async_computation | async-start | bytes 25165824 | tf_op jit(solution)/shard_map/psum | solution.py:14
  17.7 0.7 copy-start.7
  17.7 0.9 copy-start.6
  381.5 5.2 copy-start.1
  387.5 3.4 copy-start.4
  387.5 3.4 copy-start.5
  409.1 3.4 copy-start.2
  409.2 3.4 copy-start.3
  428.7 5.3 copy-start
  745.4 19.1 %copy-start.12 = (bf16[128,4,1024]{2,0,1:T(8,128)(2,1)S(1)}, bf16[128,4,1024]{2,0,1:T(8,128)(2,1)}, u32[]{:S(2)}) copy-start(bf16[128,4,1024]{2,0,1:T(8,128)(2,1)} %get-tuple-element.6) | copy-start | bytes 3145732
  764.5 18.3 %copy-start.11 = (bf16[128,4,1024]{2,0,1:T(8,128)(2,1)S(1)}, bf16[128,4,1024]{2,0,1:T(8,128)(2,1)}, u32[]{:S(2)}) copy-start(bf16[128,4,1024]{2,0,1:T(8,128)(2,1)} %get-tuple-element.7) | copy-start | bytes 3145732
  782.8 17.9 %copy-start.10 = (bf16[128,4,1024]{2,0,1:T(8,128)(2,1)S(1)}, bf16[128,4,1024]{2,0,1:T(8,128)(2,1)}, u32[]{:S(2)}) copy-start(bf16[128,4,1024]{2,0,1:T(8,128)(2,1)} %get-tuple-element.8) | copy-start | bytes 3145732
  800.7 18.3 %copy-start.9 = (bf16[128,4,1024]{2,0,1:T(8,128)(2,1)S(1)}, bf16[128,4,1024]{2,0,1:T(8,128)(2,1)}, u32[]{:S(2)}) copy-start(bf16[128,4,1024]{2,0,1:T(8,128)(2,1)} %get-tuple-element.9) | copy-start | bytes 3145732
  819.0 17.8 %copy-start.8 = (bf16[128,4,1024]{2,0,1:T(8,128)(2,1)S(1)}, bf16[128,4,1024]{2,0,1:T(8,128)(2,1)}, u32[]{:S(2)}) copy-start(bf16[128,4,1024]{2,0,1:T(8,128)(2,1)} %get-tuple-element.10) | copy-start | bytes 3145732
Sparse Core Ops, SparseCore 0:
  17.8 350.5 all-reduce.4
where the time goes:
time: 880 us; the launch traced here: 870 us
  waiting for transfers between devices  349 us (40%)
  blocking collectives  234 us (27%)
  matrix products  150 us (17%)
  local copies, waits for them, and re-layouts  87.8 us (10%)
  other arithmetic  31.1 us (4%)
  between operations  18 us (2%)
    psum x1, waiting for transfers between devices, spread(): return lax.psum(block, axis)  349 us
    psum x1, blocking collectives, shards(): summed = lax.psum(cross_stack, 'win')  234 us
    dot_general x6, matrix products, project(): jnp.dot(stack_rounded.reshape(sources * receivers, width), lag_table, pre...  109 us
    dot_general x24, local copies, waits for them, and re-layouts, contract(): jnp.einsum('wkf,wrf->krf', left, right, preferred_element_type=jnp.float32)  52.2 us
    dot_general x24, matrix products, contract(): jnp.einsum('wkf,wrf->krf', left, right, preferred_element_type=jnp.float32)  40.4 us
  transfers between devices with their start and end apart: 1, of which 1 were waited for; matrix products, arithmetic and copies ran while one was open for 0% of the time, Pallas kernels for 0%

commit v1 on v0

v1 whole, which is shorter than its diff:
```python
import functools
import math

import jax
import jax.numpy as jnp
from jax import lax
from jax.experimental import pallas as pl
from jax.experimental.pallas import tpu as pltpu
from jax.sharding import PartitionSpec as P

LAGS = 4096
STEPS = 6
FREQ = 512
SRC = 128
HOLDERS = 32
LOCAL_WIN = 8
FINE = 8
VMEM_LIMIT = 48 * 1024 * 1024
F32 = jnp.float32
BF16 = jnp.bfloat16
CORE_SWAP = [(0, 1), (1, 0), (2, 3), (3, 2)]
HALF_SWAP = [(0, 2), (1, 3), (2, 0), (3, 1)]


def params():
    return pltpu.CompilerParams(vmem_limit_bytes=VMEM_LIMIT)


def pack_kernel(re_ref, im_ref, rec_re_ref, rec_im_ref, out_ref, tall, small):
    for part, ref in enumerate((re_ref, im_ref)):
        for w in range(LOCAL_WIN):
            tall[pl.ds(part * LOCAL_WIN + w, 128, stride=16), :] = ref[w].astype(F32).T
    for part, ref in enumerate((rec_re_ref, rec_im_ref)):
        block = jnp.concatenate([ref[...], jnp.zeros((96, 128), BF16)], axis=0)
        small[pl.ds(part, 128, stride=2), :] = block.astype(F32).T
    out_ref[:, :, :128, :] = tall[...].reshape(8, 2, 128, 128).astype(BF16)
    out_ref[:, :, 128:, :] = small[...].reshape(8, 2, 16, 128).astype(BF16)


def pack(source_spectra, masked):
    spec_re = pl.BlockSpec((LOCAL_WIN, SRC, 128), lambda b: (0, 0, b))
    spec_im = pl.BlockSpec((LOCAL_WIN, SRC, 128), lambda b: (0, 0, b + 4))
    rec_re = pl.BlockSpec((32, 128), lambda b: (0, b))
    rec_im = pl.BlockSpec((32, 128), lambda b: (0, b + 4))
    return pl.pallas_call(
        pack_kernel,
        grid=(4,),
        in_specs=[spec_re, spec_im, rec_re, rec_im],
        out_specs=pl.BlockSpec((8, 2, 144, 128), lambda b: (b, 0, 0, 0)),
        out_shape=jax.ShapeDtypeStruct((HOLDERS, 2, 144, 128), BF16),
        scratch_shapes=[pltpu.VMEM((2048, 128), F32), pltpu.VMEM((256, 128), F32)],
        compiler_params=params(),
    )(source_spectra, source_spectra, masked, masked)


def select_kernel(plan, block_ref, rec_ref, mine_ref, other_ref, spread):
    step = pl.program_id(0)
    core = plan[STEPS]

    @pl.when(step < STEPS)
    def _():
        mine_ref[0] = block_ref[0, core, :128, :]
        other_ref[0] = block_ref[0, 1 - core, :128, :]

    @pl.when(step == STEPS)
    def _():
        flat = rec_ref[...].reshape(HOLDERS * 32, 128)
        row = lax.broadcasted_iota(jnp.int32, (128, 128), 0)
        lane = lax.broadcasted_iota(jnp.int32, (128, 128), 1)
        holder = lax.broadcasted_iota(jnp.int32, (HOLDERS, 32, 128), 0)
        own = lax.broadcasted_iota(jnp.int32, (HOLDERS, 32, 128), 2) // 4 == holder
        for w in range(LOCAL_WIN):
            place = jnp.where(row == 4 * w + lane % 4, 1.0, 0.0).astype(BF16)
            tiled = jnp.dot(flat, place, preferred_element_type=F32).reshape(HOLDERS, 32, 128)
            spread[pl.ds(w, 32, stride=LOCAL_WIN), :] = jnp.sum(jnp.where(own, tiled, 0.0), axis=0)
        mine_ref[0] = spread[pl.ds(pl.multiple_of(core * 128, 128), 128), :].astype(BF16)
        other_ref[0] = spread[pl.ds(pl.multiple_of((1 - core) * 128, 128), 128), :].astype(BF16)


def select(plan, blocks):
    shape = jax.ShapeDtypeStruct((STEPS + 1, 128, 128), BF16)
    return pl.pallas_call(
        select_kernel,
        grid_spec=pltpu.PrefetchScalarGridSpec(
            num_scalar_prefetch=1,
            grid=(STEPS + 1,),
            in_specs=[
                pl.BlockSpec((1, 2, 144, 128), lambda s, plan: (plan[jnp.minimum(s, STEPS - 1)], 0, 0, 0)),
                pl.BlockSpec((HOLDERS, 2, 16, 128), lambda s, plan: (0, 0, 8, 0)),
            ],
            out_specs=[pl.BlockSpec((1, 128, 128), lambda s, plan: (s, 0, 0))] * 2,
            scratch_shapes=[pltpu.VMEM((256, 128), F32)],
        ),
        out_shape=[shape, shape],
        compiler_params=params(),
    )(plan, blocks, blocks)


def stack_kernel(a_ref, b_ref, c_ref, d_ref, out_ref, weights, tall):
    step = pl.program_id(0)
    groups = (a_ref, b_ref, c_ref, d_ref)

    @pl.when(step == 0)
    def _():
        for i in range(FINE):
            real, imag = [], []
            for ref in groups:
                tile = ref[STEPS, 16 * i : 16 * i + 16, :].astype(F32)
                real += [tile]
                imag += [-tile[8:], tile[:8]]
            both = jnp.concatenate([jnp.concatenate(real, axis=0), jnp.concatenate(imag, axis=0)], axis=1)
            weights[i] = both.T.astype(BF16)

    for i in range(FINE):
        block = jnp.concatenate([ref[step, 16 * i : 16 * i + 16, :] for ref in groups], axis=0)
        both = jnp.dot(weights[i], block, preferred_element_type=F32)
        tall[pl.ds(i, 128, stride=16), :] = both[:128]
        tall[pl.ds(FINE + i, 128, stride=16), :] = both[128:]
    out_ref[:, 0] = tall[...].reshape(HOLDERS, 64, 128).astype(BF16)


def stack(groups):
    whole = pl.BlockSpec((STEPS + 1, 128, 128), lambda s: (0, 0, 0))
    return pl.pallas_call(
        stack_kernel,
        grid=(STEPS,),
        in_specs=[whole] * 4,
        out_specs=pl.BlockSpec((HOLDERS, 1, 64, 128), lambda s: (0, s, 0, 0)),
        out_shape=jax.ShapeDtypeStruct((HOLDERS, STEPS, 64, 128), BF16),
        scratch_shapes=[pltpu.VMEM((FINE, 256, 64), BF16), pltpu.VMEM((2048, 128), F32)],
        compiler_params=params(),
    )(*groups)


def project_kernel(own_ref, far_ref, own_table, far_table, taper_ref, out_ref, tall):
    for r in range(4):
        rows = slice(16 * r, 16 * r + 16)
        own = own_ref[:, 0, rows, :].reshape(512, 128)
        far = far_ref[:, 0, rows, :].reshape(512, 128)
        dims = (((0,), (0,)), ((), ()))
        total = lax.dot_general(own, own_table[...], dims, preferred_element_type=F32)
        total += lax.dot_general(far, far_table[...], dims, preferred_element_type=F32)
        total = total * taper_ref[...]
        for b in range(0, total.shape[1], 128):
            tall[b // 128, pl.ds(r, 128, stride=4), :] = total[:, b : b + 128]
    for b in range(0, out_ref.shape[3], 128):
        out_ref[0, :, :, b : b + 128] = tall[b // 128].reshape(128, 4, 128).astype(BF16)


def project(own, far, own_table, far_table, taper):
    count = own_table.shape[1]
    block = pl.BlockSpec((HOLDERS, 1, 64, 128), lambda s: (0, s, 0, 0))
    table = pl.BlockSpec((512, count), lambda s: (0, 0))
    return pl.pallas_call(
        project_kernel,
        grid=(STEPS,),
        in_specs=[block, block, table, table, pl.BlockSpec((1, count), lambda s: (0, 0))],
        out_specs=pl.BlockSpec((1, SRC, 4, count), lambda s: (s, 0, 0, 0)),
        out_shape=jax.ShapeDtypeStruct((STEPS, SRC, 4, count), BF16),
        scratch_shapes=[pltpu.VMEM((count // 128, 512, 128), F32)],
        compiler_params=params(),
    )(own, far, own_table, far_table, taper)


def waves(wave, shift):
    angle = (wave[:, None] * shift[None, :] % (2 * LAGS)).astype(F32) * (math.pi / LAGS)
    return jnp.cos(angle), jnp.sin(angle)


def build_tables(start, count, core, scale):
    shift = jnp.arange(count, dtype=jnp.int32) + start - LAGS // 2
    fine_cos, fine_sin = waves(jnp.arange(FINE, dtype=jnp.int32), shift)
    tables = []
    for h in (core, 1 - core):
        coarse = 16 * jnp.arange(HOLDERS, dtype=jnp.int32) + FREQ // 8 + 8 * h
        cos, sin = waves(coarse, shift)
        cos, sin = cos[:, None, :] * scale, sin[:, None, :] * scale
        real = cos * fine_cos - sin * fine_sin
        imag = -(sin * fine_cos + cos * fine_sin)
        tables.append(jnp.stack([real, imag], axis=1).astype(BF16).reshape(512, count))
    return tables


def build_taper(start, count):
    position = jnp.arange(count, dtype=jnp.int32) + start
    edge = jnp.minimum(position, LAGS - 1 - position) + 1
    return jnp.minimum(1.0, edge.astype(F32) / (LAGS // 16))


def shards(source_spectra, receiver_spectra, quality_mask, owner_plan):
    win = lax.axis_index("win")
    core = win % 2
    count = LAGS // 4
    scale = 1.0 / math.sqrt(FREQ * LOCAL_WIN * 4)
    own_table, far_table = build_tables(win * count, count, core, scale)
    taper = build_taper(win * count, count)[None, :]
    masked = (receiver_spectra * quality_mask.astype(BF16)[:, :, None]).reshape(32, 2 * FREQ)
    packed = pack(source_spectra, masked)
    held = lax.all_to_all(packed, "chan", 0, 0, tiled=True)
    plan = jnp.concatenate([owner_plan, core[None].astype(jnp.int32)])
    mine, other = select(plan, held)
    from_core = lax.ppermute(other, "win", CORE_SWAP)
    from_half = lax.ppermute(mine, "win", HALF_SWAP)
    from_both = lax.ppermute(from_core, "win", HALF_SWAP)
    stacked = stack([mine, from_core, from_half, from_both])
    own = lax.all_to_all(stacked, "chan", 0, 0, tiled=True)
    far = lax.ppermute(own, "win", CORE_SWAP)
    return project(own, far, own_table, far_table, taper)


def solution(mesh):
    return jax.shard_map(
        shards,
        mesh=mesh,
        in_specs=(P("win", "chan", None), P("win", "chan", None), P("win", "chan"), P()),
        out_specs=P(None, None, "chan", "win"),
        check_vma=False,
    )
```

time: 880 us -> 131 us (0.15); the launches traced: 870 us -> 131 us
  waiting for transfers between devices: 349 us -> 44.2 us
  blocking collectives: 234 us -> 42.4 us
  matrix products: 150 us -> 0 us
  local copies, waits for them, and re-layouts: 87.8 us -> 3.11 us
  other arithmetic: 31.1 us -> 3.81 us
  Pallas kernels: 0 us -> 19.5 us
  between operations: 18 us -> 0.12 us
  starting transfers between devices: 0.01 us -> 17.7 us
    psum x1 -> x0, waiting for transfers between devices: 349 us -> none  [spread(): return lax.psum(block, axis)]
    psum x1 -> x0, blocking collectives: 234 us -> none  [shards(): summed = lax.psum(cross_stack, 'win')]
    dot_general x30 -> x0, matrix products: 150 us -> none  [the longest x6 109 us: project(): jnp.dot(stack_rounded.reshape(sources * receivers, width), lag_table, pre...]
    dot_general x24 -> x0, local copies, waits for them, and re-layouts: 52.2 us -> none  [contract(): jnp.einsum('wkf,wrf->krf', left, right, preferred_element_type=jnp.float32)]
    all_to_all x0 -> x1, blocking collectives: none -> 42.4 us  [shards(): own = lax.all_to_all(stacked, 'chan', 0, 0, tiled=True)]
    all_to_all x0 -> x1, waiting for transfers between devices: none -> 30.9 us  [shards(): held = lax.all_to_all(packed, 'chan', 0, 0, tiled=True)]
    slice x19 -> x0, local copies, waits for them, and re-layouts: 27.2 us -> none  [the longest x9 13.9 us: cross_spectra(): src_real = source_block[:, :, :bin_count]]
    pallas_call x0 -> x4, Pallas kernels: none -> 19.5 us  [the longest x1 11.9 us: project(): pl.pallas_call(project_kernel, grid=(STEPS,), in_specs=[block, block, tab...]
  transfers between devices with their start and end apart: 1 -> 5, of which waited for: 1 -> 4; matrix products, arithmetic and copies ran while one was open for 0% -> 2% of each run, Pallas kernels for 0% -> 0%
where the time goes in v1:
time: 131 us
  waiting for transfers between devices  44.2 us (34%)
  blocking collectives  42.4 us (32%)
  Pallas kernels  19.5 us (15%)
  starting transfers between devices  17.7 us (14%)
  other arithmetic  3.81 us (3%)
  local copies, waits for them, and re-layouts  3.11 us (2%)
    all_to_all x1, blocking collectives, shards(): own = lax.all_to_all(stacked, 'chan', 0, 0, tiled=True)  42.4 us
    all_to_all x1, waiting for transfers between devices, shards(): held = lax.all_to_all(packed, 'chan', 0, 0, tiled=True)  30.9 us
    pallas_call x1, Pallas kernels, project(): pl.pallas_call(project_kernel, grid=(STEPS,), in_specs=[block, block, tab...  11.9 us
    all_to_all x1, starting transfers between devices, shards(): held = lax.all_to_all(packed, 'chan', 0, 0, tiled=True)  9.94 us
    ppermute x1, waiting for transfers between devices, shards(): from_half = lax.ppermute(mine, 'win', HALF_SWAP)  5.1 us
    ppermute x1, waiting for transfers between devices, shards(): from_both = lax.ppermute(from_core, 'win', HALF_SWAP)  4.91 us
    pallas_call x1, Pallas kernels, stack(): pl.pallas_call(stack_kernel, grid=(STEPS,), in_specs=[whole] * 4, out_spe...  3.8 us
    ppermute x1, waiting for transfers between devices, shards(): far = lax.ppermute(own, 'win', CORE_SWAP)  3.27 us
  transfers between devices with their start and end apart: 5, of which 4 were waited for; matrix products, arithmetic and copies ran while one was open for 2% of the time, Pallas kernels for 0%

profile of v1, /device:TPU:1, one launch (start us, length us, event | category | flops | bytes accessed | tf_op | source)
XLA Modules:
  0.0 130.8 jit_solution(15177867269749386704)
XLA Ops:
  0.0 0.7 convert_element_type.53
  0.7 0.1 copy.5
  0.8 0.9 broadcast_multiply_fusion
  1.7 0.0 copy-start.1
  1.8 1.6 %copy-done.1 = bf16[8,128,1024]{2,1,0:T(8,128)(2,1)S(1)} copy-done((bf16[8,128,1024]{2,1,0:T(8,128)(2,1)S(1)}, bf16[8,128,1024]{2,1,0:T(8,128)(2,1)}, u32[]{:S(2)}) %copy-start.1) | copy-done | bytes 2097176
  3.3 2.3 %shard_map.46 = bf16[32,2,144,128]{3,2,1,0:T(8,128)(2,1)S(1)} custom-call(bf16[8,128,1024]{2,1,0:T(8,128)(2,1)S(1)} %copy-done.1, bf16[8,128,1024]{2,1,0:T(8,128)(2,1)S(1)} %copy-done.1, bf16[32,1024]{1,0:T(8,128)(2,1)S(1)} %reshape.270.rec_re_ref.rec_im_ref, bf16[32,1024]{1,0:T(8,128)(2,1)S(1)} %reshape.270.rec_re_ref.rec_im_ref), custom_call_target="tpu_custom_call" | custom-call | tf_op jit(solution)/shard_map/pallas_call | solution.py:45
  5.7 0.0 copy-start
  5.7 1.4 %copy-done = bf16[32,2,144,128]{3,2,1,0:T(8,128)(2,1)} copy-done((bf16[32,2,144,128]{3,2,1,0:T(8,128)(2,1)}, bf16[32,2,144,128]{3,2,1,0:T(8,128)(2,1)S(1)}, u32[]{:S(2)}) %copy-start) | copy-done | bytes 2359320
  7.1 0.0 copy-start.2
  7.1 9.9 %all-to-all-start = ((bf16[32,2,144,128]{3,2,1,0:T(8,128)(2,1)}), bf16[32,2,144,128]{3,2,1,0:T(8,128)(2,1)S(1)}, u32[]{:S(2)}, u32[]{:S(2)}) async-start(bf16[32,2,144,128]{3,2,1,0:T(8,128)(2,1)} %copy-done), calls=%async_computation | async-start | bytes 4718592 | tf_op jit(solution)/shard_map/all_to_all | solution.py:199
  17.1 0.0 copy-done.2
  17.1 0.1 pad_add_fusion.plan
  17.1 30.9 %all-to-all-done.block_ref.rec_ref = bf16[32,2,144,128]{3,2,1,0:T(8,128)(2,1)S(1)} async-done(((bf16[32,2,144,128]{3,2,1,0:T(8,128)(2,1)}), bf16[32,2,144,128]{3,2,1,0:T(8,128)(2,1)S(1)}, u32[]{:S(2)}, u32[]{:S(2)}) %all-to-all-start) | async-done | bytes 2359328 | tf_op jit(solution)/shard_map/all_to_all | solution.py:199
  48.0 1.5 %shard_map.47 = (bf16[7,128,128]{2,1,0:T(8,128)(2,1)S(1)}, bf16[7,128,128]{2,1,0:T(8,128)(2,1)S(1)}) custom-call(s32[7]{0:T(128)S(1)} %pad_add_fusion.plan, bf16[32,2,144,128]{3,2,1,0:T(8,128)(2,1)S(1)} %all-to-all-done.block_ref.rec_ref, bf16[32,2,144,128]{3,2,1,0:T(8,128)(2,1)S(1)} %all-to-all-done.block_ref.rec_ref), custom_call_target="tpu_custom_call" | custom-call | tf_op jit(solution)/shard_map/pallas_call | solution.py:82
  49.5 2.1 %collective-permute-start = (bf16[7,128,128]{2,1,0:T(8,128)(2,1)S(1)}, bf16[7,128,128]{2,1,0:T(8,128)(2,1)S(1)}, u32[]{:S(2)}, u32[]{:S(2)}) collective-permute-start(bf16[7,128,128]{2,1,0:T(8,128)(2,1)S(1)} %get-tuple-element.8), channel_id=1, source_target_pairs={{0,32},{32,0},{64,96},{96,64},{1,33},{33,1},{65,97},{97,65},{2,34}... | collective-permute-start | bytes 688136 | tf_op jit(solution)/shard_map/ppermute | solution.py:202
  51.6 2.5 %collective-permute-start.1 = (bf16[7,128,128]{2,1,0:T(8,128)(2,1)S(1)}, bf16[7,128,128]{2,1,0:T(8,128)(2,1)S(1)}, u32[]{:S(2)}, u32[]{:S(2)}) collective-permute-start(bf16[7,128,128]{2,1,0:T(8,128)(2,1)S(1)} %get-tuple-element.7.a_ref), channel_id=1, source_target_pairs={{0,64},{32,96},{64,0},{96,32},{1,65},{33,97},{65,1},{97,33},{2,66}... | collective-permute-start | bytes 688136 | tf_op jit(solution)/shard_map/ppermute | solution.py:203
  54.1 0.0 collective-permute-done.b_ref
  54.1 1.1 collective-permute-start.2
  55.2 5.1 %collective-permute-done.1.c_ref = bf16[7,128,128]{2,1,0:T(8,128)(2,1)S(1)} collective-permute-done((bf16[7,128,128]{2,1,0:T(8,128)(2,1)S(1)}, bf16[7,128,128]{2,1,0:T(8,128)(2,1)S(1)}, u32[]{:S(2)}, u32[]{:S(2)}) %collective-permute-start.1) | collective-permute-done | bytes 229408 | tf_op jit(solution)/shard_map/ppermute | solution.py:203
  60.3 4.9 %collective-permute-done.2.d_ref = bf16[7,128,128]{2,1,0:T(8,128)(2,1)S(1)} collective-permute-done((bf16[7,128,128]{2,1,0:T(8,128)(2,1)S(1)}, bf16[7,128,128]{2,1,0:T(8,128)(2,1)S(1)}, u32[]{:S(2)}, u32[]{:S(2)}) %collective-permute-start.2) | collective-permute-done | bytes 229408 | tf_op jit(solution)/shard_map/ppermute | solution.py:204
  65.2 3.8 %shard_map.48 = bf16[32,6,64,128]{3,2,1,0:T(8,128)(2,1)S(1)} custom-call(bf16[7,128,128]{2,1,0:T(8,128)(2,1)S(1)} %get-tuple-element.7.a_ref, bf16[7,128,128]{2,1,0:T(8,128)(2,1)S(1)} %collective-permute-done.b_ref, bf16[7,128,128]{2,1,0:T(8,128)(2,1)S(1)} %collective-permute-done.1.c_ref, bf16[7,128,128]{2,1,0:T(8,128)(2,1)S(1)} %collective-permute-done.2.d_ref), custom_call_target="tpu_custom_call" | custom-call | tf_op jit(solution)/shard_map/pallas_call | solution.py:124
  69.0 42.4 %all_to_all.10.own_ref = bf16[32,6,64,128]{3,2,1,0:T(8,128)(2,1)S(1)} all-to-all(bf16[32,6,64,128]{3,2,1,0:T(8,128)(2,1)S(1)} %shard_map.48), channel_id=1, replica_groups=mesh['win'=4,'chan'=32] {'chan'}, dimensions={0} | all-to-all | bytes 6291456 | tf_op jit(solution)/shard_map/all_to_all | solution.py:206
  111.4 2.1 %collective-permute-start.3 = (bf16[32,6,64,128]{3,2,1,0:T(8,128)(2,1)S(1)}, bf16[32,6,64,128]{3,2,1,0:T(8,128)(2,1)}, u32[]{:S(2)}, u32[]{:S(2)}) collective-permute-start(bf16[32,6,64,128]{3,2,1,0:T(8,128)(2,1)S(1)} %all_to_all.10.own_ref), channel_id=1, source_target_pairs={{0,32},{32,0},{64,96},{96,64},{1,33},{33,1},{65,97},{97,65},{2,34}... | collective-permute-start | bytes 9437192 | tf_op jit(solution)/shard_map/ppermute | solution.py:207
  113.5 0.1 fusion.13
  113.7 1.1 cosine_multiply_fusion
  114.8 0.6 subtract_convert_fusion
  115.4 0.1 pad_maximum_fusion.1
  115.5 0.1 pad_maximum_fusion
  115.7 3.3 %collective-permute-done.3.far_ref = bf16[32,6,64,128]{3,2,1,0:T(8,128)(2,1)} collective-permute-done((bf16[32,6,64,128]{3,2,1,0:T(8,128)(2,1)S(1)}, bf16[32,6,64,128]{3,2,1,0:T(8,128)(2,1)}, u32[]{:S(2)}, u32[]{:S(2)}) %collective-permute-start.3) | collective-permute-done | bytes 3145760 | tf_op jit(solution)/shard_map/ppermute | solution.py:207
  118.9 11.9 %shard_map.49 = bf16[6,128,4,1024]{3,2,1,0:T(4,128)(2,1)} custom-call(bf16[32,6,64,128]{3,2,1,0:T(8,128)(2,1)S(1)} %all_to_all.10.own_ref, bf16[32,6,64,128]{3,2,1,0:T(8,128)(2,1)} %collective-permute-done.3.far_ref, bf16[512,1024]{1,0:T(8,128)(2,1)S(1)} %bitcast.4, bf16[512,1024]{1,0:T(8,128)(2,1)S(1)} %bitcast.3, f32[1,1024]{1,0:T(1,128)S(1)} %fusion.17.taper_ref), custom_call_target="tpu_custom_call" | custom-call | tf_op jit(solution)/shard_map/pallas_call | solution.py:154
  (4 shorter events, 0.0 us)
Async XLA Ops:
  1.7 1.6 %copy-start.1 = (bf16[8,128,1024]{2,1,0:T(8,128)(2,1)S(1)}, bf16[8,128,1024]{2,1,0:T(8,128)(2,1)}, u32[]{:S(2)}) copy-start(bf16[8,128,1024]{2,1,0:T(8,128)(2,1)} %im_ref.1) | copy-start | bytes 6291460
  5.7 1.4 %copy-start = (bf16[32,2,144,128]{3,2,1,0:T(8,128)(2,1)}, bf16[32,2,144,128]{3,2,1,0:T(8,128)(2,1)S(1)}, u32[]{:S(2)}) copy-start(bf16[32,2,144,128]{3,2,1,0:T(8,128)(2,1)S(1)} %shard_map.46) | copy-start | bytes 7077892
  7.1 10.0 %copy-start.2 = (s32[6]{0:T(128)S(1)}, s32[6]{0:T(128)}, u32[]{:S(2)}) copy-start(s32[6]{0:T(128)} %param.7) | copy-start | bytes 76
  7.1 40.9 %all-to-all-start = ((bf16[32,2,144,128]{3,2,1,0:T(8,128)(2,1)}), bf16[32,2,144,128]{3,2,1,0:T(8,128)(2,1)S(1)}, u32[]{:S(2)}, u32[]{:S(2)}) async-start(bf16[32,2,144,128]{3,2,1,0:T(8,128)(2,1)} %copy-done), calls=%async_computation | async-start | bytes 4718592 | tf_op jit(solution)/shard_map/all_to_all | solution.py:199
  49.5 4.6 %collective-permute-start = (bf16[7,128,128]{2,1,0:T(8,128)(2,1)S(1)}, bf16[7,128,128]{2,1,0:T(8,128)(2,1)S(1)}, u32[]{:S(2)}, u32[]{:S(2)}) collective-permute-start(bf16[7,128,128]{2,1,0:T(8,128)(2,1)S(1)} %get-tuple-element.8), channel_id=1, source_target_pairs={{0,32},{32,0},{64,96},{96,64},{1,33},{33,1},{65,97},{97,65},{2,34}... | collective-permute-start | bytes 688136 | tf_op jit(solution)/shard_map/ppermute | solution.py:202
  51.6 8.7 %collective-permute-start.1 = (bf16[7,128,128]{2,1,0:T(8,128)(2,1)S(1)}, bf16[7,128,128]{2,1,0:T(8,128)(2,1)S(1)}, u32[]{:S(2)}, u32[]{:S(2)}) collective-permute-start(bf16[7,128,128]{2,1,0:T(8,128)(2,1)S(1)} %get-tuple-element.7.a_ref), channel_id=1, source_target_pairs={{0,64},{32,96},{64,0},{96,32},{1,65},{33,97},{65,1},{97,33},{2,66}... | collective-permute-start | bytes 688136 | tf_op jit(solution)/shard_map/ppermute | solution.py:203
  54.1 11.1 %collective-permute-start.2 = (bf16[7,128,128]{2,1,0:T(8,128)(2,1)S(1)}, bf16[7,128,128]{2,1,0:T(8,128)(2,1)S(1)}, u32[]{:S(2)}, u32[]{:S(2)}) collective-permute-start(bf16[7,128,128]{2,1,0:T(8,128)(2,1)S(1)} %collective-permute-done.b_ref), channel_id=1, source_target_pairs={{0,64},{32,96},{64,0},{96,32},{1,65},{33,97},{65,1},{97,33},{2,66}... | collective-permute-start | bytes 688136 | tf_op jit(solution)/shard_map/ppermute | solution.py:204
  111.4 7.5 %collective-permute-start.3 = (bf16[32,6,64,128]{3,2,1,0:T(8,128)(2,1)S(1)}, bf16[32,6,64,128]{3,2,1,0:T(8,128)(2,1)}, u32[]{:S(2)}, u32[]{:S(2)}) collective-permute-start(bf16[32,6,64,128]{3,2,1,0:T(8,128)(2,1)S(1)} %all_to_all.10.own_ref), channel_id=1, source_target_pairs={{0,32},{32,0},{64,96},{96,64},{1,33},{33,1},{65,97},{97,65},{2,34}... | collective-permute-start | bytes 9437192 | tf_op jit(solution)/shard_map/ppermute | solution.py:207

commit v2 on v0

v2 whole, which is shorter than its diff:
```python
import functools
import math

import jax
import jax.numpy as jnp
from jax import lax
from jax.experimental import pallas as pl
from jax.experimental.pallas import tpu as pltpu
from jax.sharding import PartitionSpec as P

LAGS = 4096
STEPS = 6
FREQ = 512
SRC = 128
HOLDERS = 32
PEERS = 64
LOCAL_WIN = 8
FINE = 4
ROWS = 144
F32 = jnp.float32
BF16 = jnp.bfloat16
CORE_SWAP = [(0, 1), (1, 0), (2, 3), (3, 2)]
SAME_CORE = [[(2 * half + core) * HOLDERS + c for half in range(2) for c in range(HOLDERS)] for core in range(2)]


def params(mebibytes):
    return pltpu.CompilerParams(vmem_limit_bytes=mebibytes * 1024 * 1024)


def pack_kernel(mask_ref, re_ref, im_ref, rec_re_ref, rec_im_ref, out_ref, tall, wide, small):
    for part, ref in enumerate((re_ref, im_ref)):
        for w in range(LOCAL_WIN):
            tall[pl.ds(part * LOCAL_WIN + w, 128, stride=16), :] = ref[w].astype(F32).T
    out_ref[:, :128, :] = tall[...].reshape(16, 128, 128).astype(BF16)
    lane = lax.broadcasted_iota(jnp.int32, (1, 128), 1)
    usable = jnp.zeros((1, 128), F32)
    for w in range(LOCAL_WIN):
        for r in range(4):
            usable = jnp.where(lane == 4 * w + r, mask_ref[r, w].astype(F32), usable)
    wide[32:, :] = jnp.zeros((96, 128), F32)
    for part, ref in enumerate((rec_re_ref, rec_im_ref)):
        for w in range(LOCAL_WIN):
            wide[4 * w : 4 * w + 4, :] = ref[w].astype(F32)
        small[pl.ds(part, 128, stride=2), :] = wide[...].T * usable
    out_ref[:, 128:, :] = small[...].reshape(16, 16, 128).astype(BF16)


def pack(source_spectra, receiver_spectra, quality_mask):
    spec_re = pl.BlockSpec((LOCAL_WIN, SRC, 128), lambda b: (0, 0, b))
    spec_im = pl.BlockSpec((LOCAL_WIN, SRC, 128), lambda b: (0, 0, b + 4))
    rec_re = pl.BlockSpec((LOCAL_WIN, 4, 128), lambda b: (0, 0, b))
    rec_im = pl.BlockSpec((LOCAL_WIN, 4, 128), lambda b: (0, 0, b + 4))
    return pl.pallas_call(
        pack_kernel,
        grid=(4,),
        in_specs=[pl.BlockSpec(memory_space=pltpu.SMEM), spec_re, spec_im, rec_re, rec_im],
        out_specs=pl.BlockSpec((16, ROWS, 128), lambda b: (b, 0, 0)),
        out_shape=jax.ShapeDtypeStruct((PEERS, ROWS, 128), BF16),
        scratch_shapes=[pltpu.VMEM((2048, 128), F32), pltpu.VMEM((128, 128), F32), pltpu.VMEM((256, 128), F32)],
        compiler_params=params(60),
    )(quality_mask.T, source_spectra, source_spectra, receiver_spectra, receiver_spectra)


def select_kernel(plan, held_ref, mine_ref, other_ref, spread):
    core = lax.axis_index("win") % 2
    own = pl.ds(pl.multiple_of(64 * core, 64), 64)
    far = pl.ds(pl.multiple_of(64 * (1 - core), 64), 64)
    flat = held_ref[:, :, 128:, :].reshape(PEERS * 16, 128)
    row = lax.broadcasted_iota(jnp.int32, (128, 128), 0)
    lane = lax.broadcasted_iota(jnp.int32, (128, 128), 1)
    holder = lax.broadcasted_iota(jnp.int32, (HOLDERS, 16, 128), 0)
    here = lax.broadcasted_iota(jnp.int32, (HOLDERS, 16, 128), 2) // 4 == holder
    for w in range(LOCAL_WIN):
        place = jnp.where(row == 4 * w + lane % 4, 1.0, 0.0).astype(BF16)
        tiled = jnp.dot(flat, place, preferred_element_type=F32).reshape(2, HOLDERS, 16, 128)
        for half in range(2):
            one = jnp.sum(jnp.where(here, tiled[half], 0.0), axis=0)
            spread[half, pl.ds(w, 16, stride=LOCAL_WIN), :] = one
    for half in range(2):
        to = slice(64 * half, 64 * half + 64)
        mine_ref[0, to, :] = spread[half, own, :].astype(BF16)
        other_ref[0, to, :] = spread[half, far, :].astype(BF16)
        for step in range(STEPS):
            mine_ref[step + 1, to, :] = held_ref[half, plan[step], own, :]
            other_ref[step + 1, to, :] = held_ref[half, plan[step], far, :]


def select(plan, blocks):
    return pl.pallas_call(
        select_kernel,
        in_specs=[pl.BlockSpec(memory_space=pltpu.SMEM), pl.BlockSpec(memory_space=pltpu.VMEM)],
        out_shape=[jax.ShapeDtypeStruct((STEPS + 1, 128, 128), BF16)] * 2,
        scratch_shapes=[pltpu.VMEM((2, 128, 128), F32)],
        compiler_params=params(16),
    )(plan, blocks)


def stack_kernel(a, b, out_ref, weights, tall):
    def tiles(step, i):
        return [ref[step, 64 * half + 16 * i : 64 * half + 16 * i + 16, :] for ref in (a, b) for half in range(2)]

    for i in range(FINE):
        real, imag = [], []
        for tile in tiles(0, i):
            tile = tile.astype(F32)
            real += [tile]
            imag += [-tile[8:], tile[:8]]
        both = jnp.concatenate([jnp.concatenate(real, axis=0), jnp.concatenate(imag, axis=0)], axis=1)
        weights[i] = both.T.astype(BF16)

    @pl.loop(0, STEPS)
    def _(step):
        for i in range(FINE):
            block = jnp.concatenate(tiles(step + 1, i), axis=0)
            both = jnp.dot(weights[i], block, preferred_element_type=F32)
            tall[pl.ds(i, 128, stride=8), :] = both[:128]
            tall[pl.ds(FINE + i, 128, stride=8), :] = both[128:]
        spectra = tall[...].reshape(HOLDERS, 32, 128).astype(BF16)
        for half in range(2):
            out_ref[half, :, step] = spectra


def stack(mine, from_core):
    return pl.pallas_call(
        stack_kernel,
        out_shape=jax.ShapeDtypeStruct((2, HOLDERS, STEPS, 32, 128), BF16),
        scratch_shapes=[pltpu.VMEM((FINE, 256, 64), BF16), pltpu.VMEM((1024, 128), F32)],
        compiler_params=params(16),
    )(mine, from_core).reshape(PEERS, STEPS, 32, 128)


def wide(ref, step):
    held = ref[:, step].astype(F32)
    return jnp.concatenate([held[:, 8 * r : 8 * r + 8, :].reshape(512, 128) for r in range(4)], axis=1).astype(BF16)


def turn(block, table):
    return lax.dot_general(block, table, (((0,), (0,)), ((), ())), preferred_element_type=F32)


def begin_kernel(own_ref, table_ref, out_ref):
    @pl.loop(0, STEPS)
    def _(step):
        out_ref[step] = turn(wide(own_ref, step), table_ref[...])


def begin(own, table):
    count = table.shape[1]
    return pl.pallas_call(
        begin_kernel,
        out_shape=jax.ShapeDtypeStruct((STEPS, 512, count), F32),
        compiler_params=params(8),
        cost_estimate=pl.CostEstimate(flops=STEPS * 1_000_000_000, bytes_accessed=16_000_000, transcendentals=0),
    )(own, table)


def finish_kernel(part_ref, far_ref, table_ref, taper_ref, out_ref, tall, ready, sems):
    count = table_ref.shape[1]

    def send(step, slot):
        return pltpu.make_async_copy(ready.at[slot], out_ref.at[step], sems.at[slot])

    @pl.loop(0, STEPS)
    def _(step):
        slot = lax.rem(step, 2)
        total = (turn(wide(far_ref, step), table_ref[...]) + part_ref[step]) * taper_ref[...]
        for r in range(4):
            for b in range(0, count, 128):
                tall[b // 128, pl.ds(r, 128, stride=4), :] = total[128 * r : 128 * r + 128, b : b + 128]

        @pl.when(step >= 2)
        def _():
            send(step - 2, slot).wait()

        for b in range(0, count, 128):
            ready[slot, :, :, b : b + 128] = tall[b // 128].reshape(128, 4, 128).astype(BF16)
        send(step, slot).start()

    send(STEPS - 2, 0).wait()
    send(STEPS - 1, 1).wait()


def finish(part, far, table, taper):
    count = table.shape[1]
    return pl.pallas_call(
        finish_kernel,
        out_specs=pl.BlockSpec(memory_space=pl.ANY),
        out_shape=jax.ShapeDtypeStruct((STEPS, SRC, 4, count), BF16),
        scratch_shapes=[
            pltpu.VMEM((count // 128, 512, 128), F32),
            pltpu.VMEM((2, SRC, 4, count), BF16),
            pltpu.SemaphoreType.DMA((2,)),
        ],
        compiler_params=params(16),
        cost_estimate=pl.CostEstimate(flops=STEPS * 1_000_000_000, bytes_accessed=22_000_000, transcendentals=0),
    )(part, far, table, taper)


def table_kernel(win_ref, own_ref, far_ref, taper_ref, *, count, scale):
    start = win_ref[0] * count
    core = win_ref[0] % 2
    shift = lax.broadcasted_iota(jnp.int32, (8, count), 1) + (start - LAGS // 2)
    index = lax.broadcasted_iota(jnp.int32, (8, count), 0)

    def waves(wave):
        angle = ((wave * shift) & (2 * LAGS - 1)).astype(F32) * (math.pi / LAGS)
        return jnp.cos(angle), jnp.sin(angle)

    high_cos, high_sin = waves(64 * index + 64)
    mid_cos, mid_sin = waves(8 * index)
    low_cos, low_sin = waves(index)
    high_cos, high_sin = high_cos * scale, high_sin * scale
    for ref, h in ((own_ref, core), (far_ref, 1 - core)):
        def rows(wave):
            return jnp.where(h == 0, jnp.concatenate([wave[:4]] * 2, axis=0), jnp.concatenate([wave[4:]] * 2, axis=0))

        fine_cos, fine_sin = rows(low_cos), rows(low_sin)
        real = index < 4
        by_cos = jnp.where(real, fine_cos, -fine_sin)
        by_sin = jnp.where(real, -fine_sin, -fine_cos)
        for a in range(8):
            for b in range(8):
                cos = high_cos[a : a + 1] * mid_cos[b : b + 1] - high_sin[a : a + 1] * mid_sin[b : b + 1]
                sin = high_sin[a : a + 1] * mid_cos[b : b + 1] + high_cos[a : a + 1] * mid_sin[b : b + 1]
                ref[8 * (8 * a + b) : 8 * (8 * a + b) + 8, :] = (cos * by_cos + sin * by_sin).astype(BF16)
    position = lax.broadcasted_iota(jnp.int32, (1, count), 1) + start
    edge = jnp.minimum(position, LAGS - 1 - position) + 1
    taper_ref[...] = jnp.minimum(1.0, edge.astype(F32) / (LAGS // 16))


def build_tables(win, count, scale):
    table = jax.ShapeDtypeStruct((512, count), BF16)
    return pl.pallas_call(
        functools.partial(table_kernel, count=count, scale=scale),
        in_specs=[pl.BlockSpec(memory_space=pltpu.SMEM)],
        out_shape=[table, table, jax.ShapeDtypeStruct((1, count), F32)],
        compiler_params=params(8),
    )(win)


def shards(source_spectra, receiver_spectra, quality_mask, owner_plan):
    count = LAGS // 4
    scale = 1.0 / math.sqrt(FREQ * LOCAL_WIN * 4)
    packed = pack(source_spectra, receiver_spectra, quality_mask)
    held = exchange(packed).reshape(2, HOLDERS, ROWS, 128)
    mine, other = select(owner_plan, held)
    from_core = lax.ppermute(other, "win", CORE_SWAP)
    win, mine = lax.optimization_barrier((lax.axis_index("win")[None], mine))
    own_table, far_table, taper = build_tables(win, count, scale)
    mine, own_table = lax.optimization_barrier((mine, own_table))
    own = exchange(stack(mine, from_core))
    far = lax.ppermute(own, "win", CORE_SWAP)
    return finish(begin(own, own_table), far, far_table, taper)


def exchange(blocks):
    return lax.all_to_all(blocks, ("win", "chan"), 0, 0, tiled=True, axis_index_groups=SAME_CORE)


def solution(mesh):
    return jax.shard_map(
        shards,
        mesh=mesh,
        in_specs=(P("win", "chan", None), P("win", "chan", None), P("win", "chan"), P()),
        out_specs=P(None, None, "chan", "win"),
        check_vma=False,
    )
```

time: 880 us -> 116 us (0.13); the launches traced: 870 us -> 116 us
  waiting for transfers between devices: 349 us -> 0.71 us
  matrix products: 150 us -> 0 us
  blocking collectives: 234 us -> 89.7 us
  local copies, waits for them, and re-layouts: 87.8 us -> 0.01 us
  other arithmetic: 31.1 us -> 0 us
  Pallas kernels: 0 us -> 21.5 us
  between operations: 18 us -> 0.03 us
    psum x1 -> x0, waiting for transfers between devices: 349 us -> none  [spread(): return lax.psum(block, axis)]
    psum x1 -> x0, blocking collectives: 234 us -> none  [shards(): summed = lax.psum(cross_stack, 'win')]
    dot_general x30 -> x0, matrix products: 150 us -> none  [the longest x6 109 us: project(): jnp.dot(stack_rounded.reshape(sources * receivers, width), lag_table, pre...]
    all_to_all x0 -> x2, blocking collectives: none -> 89.7 us  [exchange(): lax.all_to_all(blocks, ('win', 'chan'), 0, 0, tiled=True, axis_index_grou...]
    dot_general x24 -> x0, local copies, waits for them, and re-layouts: 52.2 us -> none  [contract(): jnp.einsum('wkf,wrf->krf', left, right, preferred_element_type=jnp.float32)]
    slice x19 -> x0, local copies, waits for them, and re-layouts: 27.2 us -> none  [the longest x9 13.9 us: cross_spectra(): src_real = source_block[:, :, :bin_count]]
    pallas_call x0 -> x6, Pallas kernels: none -> 21.5 us  [the longest x1 8.13 us: finish(): pl.pallas_call(finish_kernel, out_specs=pl.BlockSpec(memory_space=pl.ANY)...]
    sub x6 -> x0, other arithmetic: 10.2 us -> none  [cross_spectra(): imag_part = contract(src_imag, rec_real) - contract(src_real, rec_imag)]
  transfers between devices with their start and end apart: 1 -> 2, of which waited for: 1 -> 1; matrix products, arithmetic and copies ran while one was open for 0% -> 0% of each run, Pallas kernels for 0% -> 5%
where the time goes in v2:
time: 116 us
  blocking collectives  89.7 us (77%)
  Pallas kernels  21.5 us (19%)
  starting transfers between devices  4.15 us (4%)
    all_to_all x2, blocking collectives, exchange(): lax.all_to_all(blocks, ('win', 'chan'), 0, 0, tiled=True, axis_index_grou...  89.7 us
    pallas_call x1, Pallas kernels, finish(): pl.pallas_call(finish_kernel, out_specs=pl.BlockSpec(memory_space=pl.ANY)...  8.13 us
    pallas_call x1, Pallas kernels, pack(): pl.pallas_call(pack_kernel, grid=(4,), in_specs=[pl.BlockSpec(memory_spac...  4.64 us
    pallas_call x1, Pallas kernels, begin(): pl.pallas_call(begin_kernel, out_shape=jax.ShapeDtypeStruct((STEPS, 512,...  4.58 us
    ppermute x1, starting transfers between devices, shards(): from_core = lax.ppermute(other, 'win', CORE_SWAP)  2.4 us
  transfers between devices with their start and end apart: 2, of which 1 were waited for; matrix products, arithmetic and copies ran while one was open for 0% of the time, Pallas kernels for 5%

profile of v2, /device:TPU:1, one launch (start us, length us, event | category | flops | bytes accessed | tf_op | source)
XLA Modules:
  0.0 116.0 jit_solution(15917688254773542012)
XLA Ops:
  0.0 4.6 %shard_map.46 = bf16[64,144,128]{2,1,0:T(8,128)(2,1)} custom-call(s32[4,8]{1,0:T(4,128)} %bitcast.6, bf16[8,128,1024]{2,1,0:T(8,128)(2,1)} %im_ref.1, bf16[8,128,1024]{2,1,0:T(8,128)(2,1)} %im_ref.1, bf16[8,4,1024]{2,1,0:T(4,128)(2,1)} %rec_im_ref.1, bf16[8,4,1024]{2,1,0:T(4,128)(2,1)} %rec_im_ref.1), custom_call_target="tpu_custom_call" | custom-call | tf_op jit(solution)/shard_map/pallas_call | solution.py:53
  4.6 0.0 copy-start
  4.6 44.0 %all_to_all.10 = bf16[64,144,128]{2,1,0:T(8,128)(2,1)S(1)} all-to-all(bf16[64,144,128]{2,1,0:T(8,128)(2,1)} %shard_map.46), channel_id=1, replica_groups={{0,1,2,3,4,5,6,7,8,9,10,11,12,13,14,15,16,17,18,19,20,21,22,23,24,25,26..., dimensions={0} | all-to-all | bytes 4718592 | tf_op jit(solution)/shard_map/all_to_all | solution.py:257
  48.6 0.0 copy-done
  48.6 1.2 %shard_map.47 = (bf16[7,128,128]{2,1,0:T(8,128)(2,1)S(1)}, bf16[7,128,128]{2,1,0:T(8,128)(2,1)S(1)}) custom-call(s32[6]{0:T(128)S(1)} %copy-done, bf16[2,32,144,128]{3,2,1,0:T(8,128)(2,1)S(1)} %bitcast.5), custom_call_target="tpu_custom_call" | custom-call | tf_op jit(solution)/shard_map/pallas_call | solution.py:89
  49.9 2.4 %collective-permute-start = (bf16[7,128,128]{2,1,0:T(8,128)(2,1)S(1)}, bf16[7,128,128]{2,1,0:T(8,128)(2,1)S(1)}, u32[]{:S(2)}, u32[]{:S(2)}) collective-permute-start(bf16[7,128,128]{2,1,0:T(8,128)(2,1)S(1)} %get-tuple-element.19), channel_id=1, source_target_pairs={{0,32},{32,0},{64,96},{96,64},{1,33},{33,1},{65,97},{97,65},{2,34}... | collective-permute-start | bytes 688136 | tf_op jit(solution)/shard_map/ppermute | solution.py:247
  52.3 1.2 %shard_map.48 = (bf16[512,1024]{1,0:T(8,128)(2,1)S(1)}, bf16[512,1024]{1,0:T(8,128)(2,1)S(1)}, f32[1,1024]{1,0:T(1,128)S(1)}) custom-call(s32[1]{0:T(128)} %bitcast.win_ref), custom_call_target="tpu_custom_call" | custom-call | tf_op jit(solution)/shard_map/pallas_call | solution.py:233
  53.5 0.0 collective-permute-done.b
  53.5 1.7 %shard_map.49 = bf16[2,32,6,32,128]{4,3,2,1,0:T(8,128)(2,1)S(1)} custom-call(bf16[7,128,128]{2,1,0:T(8,128)(2,1)S(1)} %get-tuple-element.18.a, bf16[7,128,128]{2,1,0:T(8,128)(2,1)S(1)} %collective-permute-done.b), custom_call_target="tpu_custom_call" | custom-call | tf_op jit(solution)/shard_map/pallas_call | solution.py:124
  55.2 45.7 %all_to_all.11.own_ref = bf16[64,6,32,128]{3,2,1,0:T(8,128)(2,1)S(1)} all-to-all(bf16[64,6,32,128]{3,2,1,0:T(8,128)(2,1)S(1)} %bitcast.4), channel_id=1, replica_groups={{0,1,2,3,4,5,6,7,8,9,10,11,12,13,14,15,16,17,18,19,20,21,22,23,24,25,26..., dimensions={0} | all-to-all | bytes 6291456 | tf_op jit(solution)/shard_map/all_to_all | solution.py:257
  100.9 1.8 %collective-permute-start.1 = (bf16[64,6,32,128]{3,2,1,0:T(8,128)(2,1)S(1)}, bf16[64,6,32,128]{3,2,1,0:T(8,128)(2,1)S(1)}, u32[]{:S(2)}, u32[]{:S(2)}) collective-permute-start(bf16[64,6,32,128]{3,2,1,0:T(8,128)(2,1)S(1)} %all_to_all.11.own_ref), channel_id=1, source_target_pairs={{0,32},{32,0},{64,96},{96,64},{1,33},{33,1},{65,97},{97,65},{2,34}... | collective-permute-start | bytes 9437192 | tf_op jit(solution)/shard_map/ppermute | solution.py:252
  102.6 4.6 %shard_map.50.part_ref = f32[6,512,1024]{2,1,0:T(8,128)S(1)} custom-call(bf16[64,6,32,128]{3,2,1,0:T(8,128)(2,1)S(1)} %all_to_all.11.own_ref, bf16[512,1024]{1,0:T(8,128)(2,1)S(1)} %get-tuple-element.20.table_ref), custom_call_target="tpu_custom_call" | custom-call | flops 6000000000 | bytes 16000000 | tf_op jit(solution)/shard_map/pallas_call | solution.py:149
  107.2 0.7 collective-permute-done.1.far_ref
  107.9 8.1 %shard_map.51 = bf16[6,128,4,1024]{3,2,1,0:T(4,128)(2,1)} custom-call(f32[6,512,1024]{2,1,0:T(8,128)S(1)} %shard_map.50.part_ref, bf16[64,6,32,128]{3,2,1,0:T(8,128)(2,1)S(1)} %collective-permute-done.1.far_ref, bf16[512,1024]{1,0:T(8,128)(2,1)S(1)} %get-tuple-element.21.table_ref, f32[1,1024]{1,0:T(1,128)S(1)} %get-tuple-element.22.taper_ref), custom_call_target="tpu_custom_call" | custom-call | flops 6000000000 | bytes 22000000 | tf_op jit(solution)/shard_map/pallas_call | solution.py:185
Async XLA Ops:
  4.6 44.0 %copy-start = (s32[6]{0:T(128)S(1)}, s32[6]{0:T(128)}, u32[]{:S(2)}) copy-start(s32[6]{0:T(128)} %plan.1) | copy-start | bytes 76
  49.9 3.6 %collective-permute-start = (bf16[7,128,128]{2,1,0:T(8,128)(2,1)S(1)}, bf16[7,128,128]{2,1,0:T(8,128)(2,1)S(1)}, u32[]{:S(2)}, u32[]{:S(2)}) collective-permute-start(bf16[7,128,128]{2,1,0:T(8,128)(2,1)S(1)} %get-tuple-element.19), channel_id=1, source_target_pairs={{0,32},{32,0},{64,96},{96,64},{1,33},{33,1},{65,97},{97,65},{2,34}... | collective-permute-start | bytes 688136 | tf_op jit(solution)/shard_map/ppermute | solution.py:247
  100.9 7.0 %collective-permute-start.1 = (bf16[64,6,32,128]{3,2,1,0:T(8,128)(2,1)S(1)}, bf16[64,6,32,128]{3,2,1,0:T(8,128)(2,1)S(1)}, u32[]{:S(2)}, u32[]{:S(2)}) collective-permute-start(bf16[64,6,32,128]{3,2,1,0:T(8,128)(2,1)S(1)} %all_to_all.11.own_ref), channel_id=1, source_target_pairs={{0,32},{32,0},{64,96},{96,64},{1,33},{33,1},{65,97},{97,65},{2,34}... | collective-permute-start | bytes 9437192 | tf_op jit(solution)/shard_map/ppermute | solution.py:252

commit v3 on v2

v3 whole, which is shorter than its diff:
```python
import functools
import math

import jax
import jax.numpy as jnp
from jax import lax
from jax.experimental import pallas as pl
from jax.experimental.pallas import tpu as pltpu
from jax.sharding import PartitionSpec as P

LAGS = 4096
STEPS = 6
FREQ = 512
SRC = 128
HOLDERS = 32
PEERS = 64
LOCAL_WIN = 8
FINE = 4
ROWS = 136
F32 = jnp.float32
BF16 = jnp.bfloat16
CORE_SWAP = [(0, 1), (1, 0), (2, 3), (3, 2)]
SAME_CORE = [[(2 * half + core) * HOLDERS + c for half in range(2) for c in range(HOLDERS)] for core in range(2)]


def params(mebibytes):
    return pltpu.CompilerParams(vmem_limit_bytes=mebibytes * 1024 * 1024)


def pack_kernel(mask_ref, re_ref, im_ref, rec_re_ref, rec_im_ref, out_ref, block):
    lane = lax.broadcasted_iota(jnp.int32, (1, 128), 1)
    usable = jnp.zeros((1, 128), F32)
    for w in range(LOCAL_WIN):
        for r in range(4):
            usable = jnp.where(lane % 32 == 4 * w + r, mask_ref[r, w].astype(F32), usable)
    block[64:, :] = jnp.zeros((64, 128), F32)
    for b in range(2):
        lanes = slice(128 * b, 128 * b + 128)
        peers = slice(16 * b, 16 * b + 16)
        for part, ref in enumerate((rec_re_ref, rec_im_ref)):
            for w in range(LOCAL_WIN):
                row = 32 * part + 4 * w
                block[row : row + 4, :] = ref[w, :, lanes].astype(F32)
        out_ref[peers, 128:, :] = (block[...].T * usable).reshape(16, 8, 128).astype(BF16)
        for part, ref in enumerate((re_ref, im_ref)):
            for w in range(0, LOCAL_WIN, 2):
                pair = [ref[w + k, :, lanes].astype(F32).T.reshape(16, 8, 128) for k in range(2)]
                row = 64 * part + 8 * w
                out_ref[peers, row : row + 16, :] = jnp.concatenate(pair, axis=1).astype(BF16)


def pack(source_spectra, receiver_spectra, quality_mask):
    return pl.pallas_call(
        pack_kernel,
        grid=(2,),
        in_specs=[
            pl.BlockSpec(memory_space=pltpu.SMEM),
            pl.BlockSpec((LOCAL_WIN, SRC, 256), lambda b: (0, 0, b)),
            pl.BlockSpec((LOCAL_WIN, SRC, 256), lambda b: (0, 0, b + 2)),
            pl.BlockSpec((LOCAL_WIN, 4, 256), lambda b: (0, 0, b)),
            pl.BlockSpec((LOCAL_WIN, 4, 256), lambda b: (0, 0, b + 2)),
        ],
        out_specs=pl.BlockSpec((32, ROWS, 128), lambda b: (b, 0, 0)),
        out_shape=jax.ShapeDtypeStruct((PEERS, ROWS, 128), BF16),
        scratch_shapes=[pltpu.VMEM((128, 128), F32)],
        compiler_params=params(60),
    )(quality_mask.T, source_spectra, source_spectra, receiver_spectra, receiver_spectra)


def select_kernel(plan, held_ref, mine_ref, other_ref, spread, chosen):
    core = lax.axis_index("win") % 2
    own = pl.ds(pl.multiple_of(64 * core, 64), 64)
    far = pl.ds(pl.multiple_of(64 * (1 - core), 64), 64)
    flat = held_ref[:, :, 128:, :].reshape(PEERS * 8, 128)
    row = lax.broadcasted_iota(jnp.int32, (128, 128), 0)
    lane = lax.broadcasted_iota(jnp.int32, (128, 128), 1)
    holder = lax.broadcasted_iota(jnp.int32, (HOLDERS, 8, 128), 0)
    here = lax.broadcasted_iota(jnp.int32, (HOLDERS, 8, 128), 2) // 4 == holder
    for k in range(2 * LOCAL_WIN):
        place = jnp.where(row == 4 * k + lane % 4, 1.0, 0.0).astype(BF16)
        tiled = jnp.dot(flat, place, preferred_element_type=F32).reshape(2, HOLDERS, 8, 128)
        for half in range(2):
            spread[half, pl.ds(k, 8, stride=16), :] = jnp.sum(jnp.where(here, tiled[half], 0.0), axis=0)
    for half in range(2):
        to = slice(64 * half, 64 * half + 64)
        mine_ref[0, to, :] = spread[half, own, :].astype(BF16)
        other_ref[0, to, :] = spread[half, far, :].astype(BF16)
        for step in range(STEPS):
            chosen[half, step] = held_ref[half, plan[step], :128, :].astype(F32)
            for i in range(FINE):
                to = slice(64 * half + 16 * i, 64 * half + 16 * i + 16)
                mine_ref[step + 1, to, :] = chosen[half, step, pl.ds(4 * core + i, 16, stride=8), :].astype(BF16)
                other_ref[step + 1, to, :] = chosen[half, step, pl.ds(4 * (1 - core) + i, 16, stride=8), :].astype(BF16)


def select(plan, blocks):
    return pl.pallas_call(
        select_kernel,
        in_specs=[pl.BlockSpec(memory_space=pltpu.SMEM), pl.BlockSpec(memory_space=pltpu.VMEM)],
        out_shape=[jax.ShapeDtypeStruct((STEPS + 1, 128, 128), BF16)] * 2,
        scratch_shapes=[pltpu.VMEM((2, 128, 128), F32), pltpu.VMEM((2, STEPS, 128, 128), F32)],
        compiler_params=params(16),
    )(plan, blocks)


def stack_kernel(a, b, out_ref, weights, tall):
    def tiles(step, i):
        return [ref[step, 64 * half + 16 * i : 64 * half + 16 * i + 16, :] for ref in (a, b) for half in range(2)]

    for i in range(FINE):
        real, imag = [], []
        for tile in tiles(0, i):
            tile = tile.astype(F32)
            real += [tile]
            imag += [-tile[8:], tile[:8]]
        both = jnp.concatenate([jnp.concatenate(real, axis=0), jnp.concatenate(imag, axis=0)], axis=1)
        weights[i] = both.T.astype(BF16)

    @pl.loop(0, STEPS, step=2)
    def _(step):
        for i in range(FINE):
            pair = [jnp.concatenate(tiles(step + 1 + k, i), axis=0) for k in range(2)]
            both = jnp.dot(weights[i], jnp.concatenate(pair, axis=1), preferred_element_type=F32)
            for k in range(2):
                tall[k, pl.ds(i, 128, stride=8), :] = both[:128, 128 * k : 128 * k + 128]
                tall[k, pl.ds(FINE + i, 128, stride=8), :] = both[128:, 128 * k : 128 * k + 128]
        for k in range(2):
            spectra = tall[k].reshape(HOLDERS, 32, 128).astype(BF16)
            for half in range(2):
                out_ref[half, :, step + k] = spectra


def stack(mine, from_core):
    return pl.pallas_call(
        stack_kernel,
        out_shape=jax.ShapeDtypeStruct((2, HOLDERS, STEPS, 32, 128), BF16),
        scratch_shapes=[pltpu.VMEM((FINE, 256, 64), BF16), pltpu.VMEM((2, 1024, 128), F32)],
        compiler_params=params(16),
    )(mine, from_core).reshape(PEERS, STEPS, 32, 128)


def arrange(ref, step, lhs):
    held = ref[:, step].astype(F32)
    for r in range(4):
        turned = held[:, 8 * r : 8 * r + 8, :].reshape(512, 128).T
        for b in range(4):
            lhs[b, pl.ds(r, 128, stride=4), :] = turned[:, 128 * b : 128 * b + 128]


def rows(lhs):
    return jnp.concatenate([lhs[b].astype(BF16) for b in range(4)], axis=1)


def begin_kernel(own_ref, table_ref, out_ref, lhs):
    @pl.loop(0, STEPS)
    def _(step):
        arrange(own_ref, step, lhs)
        out_ref[step] = jnp.dot(rows(lhs), table_ref[...], preferred_element_type=F32)


def begin(own, table):
    count = table.shape[1]
    return pl.pallas_call(
        begin_kernel,
        out_shape=jax.ShapeDtypeStruct((STEPS, 512, count), F32),
        scratch_shapes=[pltpu.VMEM((4, 512, 128), F32)],
        compiler_params=params(8),
        cost_estimate=pl.CostEstimate(flops=STEPS * 1_000_000_000, bytes_accessed=16_000_000, transcendentals=0),
    )(own, table)


def finish_kernel(part_ref, far_ref, table_ref, taper_ref, out_ref, even, odd, ready, sems):
    count = table_ref.shape[1]
    lhs = (even, odd)

    def send(step, slot):
        return pltpu.make_async_copy(ready.at[slot], out_ref.at[step], sems.at[slot])

    arrange(far_ref, 0, even)

    @pl.loop(0, STEPS, step=2)
    def _(first):
        for slot in range(2):
            step = first + slot
            block = rows(lhs[slot])

            @pl.when(step >= 2)
            def _():
                send(step - 2, slot).wait()

            for n in range(0, count, 256):
                lags = slice(n, n + 256)
                total = jnp.dot(block, table_ref[:, lags], preferred_element_type=F32) + part_ref[step, :, lags]
                ready[slot, :, :, lags] = (total * taper_ref[:, lags]).reshape(SRC, 4, 256).astype(BF16)
            arrange(far_ref, jnp.minimum(step + 1, STEPS - 1), lhs[1 - slot])
            send(step, slot).start()

    send(STEPS - 2, 0).wait()
    send(STEPS - 1, 1).wait()


def finish(part, far, table, taper):
    count = table.shape[1]
    return pl.pallas_call(
        finish_kernel,
        out_specs=pl.BlockSpec(memory_space=pl.ANY),
        out_shape=jax.ShapeDtypeStruct((STEPS, SRC, 4, count), BF16),
        scratch_shapes=[
            pltpu.VMEM((4, 512, 128), F32),
            pltpu.VMEM((4, 512, 128), F32),
            pltpu.VMEM((2, SRC, 4, count), BF16),
            pltpu.SemaphoreType.DMA((2,)),
        ],
        compiler_params=params(16),
        cost_estimate=pl.CostEstimate(flops=STEPS * 1_000_000_000, bytes_accessed=22_000_000, transcendentals=0),
    )(part, far, table, taper)


def table_kernel(win_ref, own_ref, far_ref, taper_ref, *, count, scale):
    start = win_ref[0] * count
    core = win_ref[0] % 2
    shift = lax.broadcasted_iota(jnp.int32, (8, count), 1) + (start - LAGS // 2)
    index = lax.broadcasted_iota(jnp.int32, (8, count), 0)

    def waves(wave):
        angle = ((wave * shift) & (2 * LAGS - 1)).astype(F32) * (math.pi / LAGS)
        return jnp.cos(angle), jnp.sin(angle)

    high_cos, high_sin = waves(64 * index + 64)
    mid_cos, mid_sin = waves(8 * index)
    low_cos, low_sin = waves(index)
    high_cos, high_sin = high_cos * scale, high_sin * scale
    for ref, h in ((own_ref, core), (far_ref, 1 - core)):
        def rows(wave):
            return jnp.where(h == 0, jnp.concatenate([wave[:4]] * 2, axis=0), jnp.concatenate([wave[4:]] * 2, axis=0))

        fine_cos, fine_sin = rows(low_cos), rows(low_sin)
        real = index < 4
        by_cos = jnp.where(real, fine_cos, -fine_sin)
        by_sin = jnp.where(real, -fine_sin, -fine_cos)
        for a in range(8):
            for b in range(8):
                cos = high_cos[a : a + 1] * mid_cos[b : b + 1] - high_sin[a : a + 1] * mid_sin[b : b + 1]
                sin = high_sin[a : a + 1] * mid_cos[b : b + 1] + high_cos[a : a + 1] * mid_sin[b : b + 1]
                ref[8 * (8 * a + b) : 8 * (8 * a + b) + 8, :] = (cos * by_cos + sin * by_sin).astype(BF16)
    position = lax.broadcasted_iota(jnp.int32, (1, count), 1) + start
    edge = jnp.minimum(position, LAGS - 1 - position) + 1
    taper_ref[...] = jnp.minimum(1.0, edge.astype(F32) / (LAGS // 16))


def build_tables(win, count, scale):
    table = jax.ShapeDtypeStruct((512, count), BF16)
    return pl.pallas_call(
        functools.partial(table_kernel, count=count, scale=scale),
        in_specs=[pl.BlockSpec(memory_space=pltpu.SMEM)],
        out_shape=[table, table, jax.ShapeDtypeStruct((1, count), F32)],
        compiler_params=params(8),
    )(win)


def shards(source_spectra, receiver_spectra, quality_mask, owner_plan):
    count = LAGS // 4
    scale = 1.0 / math.sqrt(FREQ * LOCAL_WIN * 4)
    packed = pack(source_spectra, receiver_spectra, quality_mask)
    held = exchange(packed).reshape(2, HOLDERS, ROWS, 128)
    mine, other = select(owner_plan, held)
    from_core = lax.ppermute(other, "win", CORE_SWAP)
    win, mine = lax.optimization_barrier((lax.axis_index("win")[None], mine))
    own_table, far_table, taper = build_tables(win, count, scale)
    mine, own_table = lax.optimization_barrier((mine, own_table))
    own = exchange(stack(mine, from_core))
    far = lax.ppermute(own, "win", CORE_SWAP)
    return finish(begin(own, own_table), far, far_table, taper)


def exchange(blocks):
    return lax.all_to_all(blocks, ("win", "chan"), 0, 0, tiled=True, axis_index_groups=SAME_CORE)


def solution(mesh):
    return jax.shard_map(
        shards,
        mesh=mesh,
        in_specs=(P("win", "chan", None), P("win", "chan", None), P("win", "chan"), P()),
        out_specs=P(None, None, "chan", "win"),
        check_vma=False,
    )
```

time: 116 us -> 112 us (0.966)
  Pallas kernels: 21.5 us -> 19 us
    pallas_call x1, Pallas kernels: 4.64 us -> 3.02 us  [pack(): pl.pallas_call(pack_kernel, grid=(2,), in_specs=[pl.BlockSpec(memory_spac...]
where the time goes in v3:
time: 112 us
  blocking collectives  88.8 us (79%)
  Pallas kernels  19 us (17%)
  starting transfers between devices  3.76 us (3%)
    all_to_all x2, blocking collectives, exchange(): lax.all_to_all(blocks, ('win', 'chan'), 0, 0, tiled=True, axis_index_grou...  88.8 us
    pallas_call x1, Pallas kernels, finish(): pl.pallas_call(finish_kernel, out_specs=pl.BlockSpec(memory_space=pl.ANY)...  7.11 us
    pallas_call x1, Pallas kernels, begin(): pl.pallas_call(begin_kernel, out_shape=jax.ShapeDtypeStruct((STEPS, 512,...  4.85 us
    pallas_call x1, Pallas kernels, pack(): pl.pallas_call(pack_kernel, grid=(2,), in_specs=[pl.BlockSpec(memory_spac...  3.02 us
  transfers between devices with their start and end apart: 2, of which 1 were waited for; matrix products, arithmetic and copies ran while one was open for 0% of the time, Pallas kernels for 5%

profile of v3, /device:TPU:1, one launch (start us, length us, event | category | flops | bytes accessed | tf_op | source)
XLA Modules:
  0.0 112.1 jit_solution(282694265277890199)
XLA Ops:
  0.0 3.0 %shard_map.46 = bf16[64,136,128]{2,1,0:T(8,128)(2,1)} custom-call(s32[4,8]{1,0:T(4,128)} %bitcast.6, bf16[8,128,1024]{2,1,0:T(8,128)(2,1)} %im_ref.1, bf16[8,128,1024]{2,1,0:T(8,128)(2,1)} %im_ref.1, bf16[8,4,1024]{2,1,0:T(4,128)(2,1)} %rec_im_ref.1, bf16[8,4,1024]{2,1,0:T(4,128)(2,1)} %rec_im_ref.1), custom_call_target="tpu_custom_call" | custom-call | tf_op jit(solution)/shard_map/pallas_call | solution.py:53
  3.0 0.0 copy-start
  3.0 43.3 %all_to_all.10 = bf16[64,136,128]{2,1,0:T(8,128)(2,1)S(1)} all-to-all(bf16[64,136,128]{2,1,0:T(8,128)(2,1)} %shard_map.46), channel_id=1, replica_groups={{0,1,2,3,4,5,6,7,8,9,10,11,12,13,14,15,16,17,18,19,20,21,22,23,24,25,26..., dimensions={0} | all-to-all | bytes 4456448 | tf_op jit(solution)/shard_map/all_to_all | solution.py:277
  46.3 0.0 copy-done
  46.3 1.5 %shard_map.47 = (bf16[7,128,128]{2,1,0:T(8,128)(2,1)S(1)}, bf16[7,128,128]{2,1,0:T(8,128)(2,1)S(1)}) custom-call(s32[6]{0:T(128)S(1)} %copy-done, bf16[2,32,136,128]{3,2,1,0:T(8,128)(2,1)S(1)} %bitcast.5), custom_call_target="tpu_custom_call" | custom-call | tf_op jit(solution)/shard_map/pallas_call | solution.py:97
  47.8 2.0 %collective-permute-start = (bf16[7,128,128]{2,1,0:T(8,128)(2,1)S(1)}, bf16[7,128,128]{2,1,0:T(8,128)(2,1)S(1)}, u32[]{:S(2)}, u32[]{:S(2)}) collective-permute-start(bf16[7,128,128]{2,1,0:T(8,128)(2,1)S(1)} %get-tuple-element.19), channel_id=1, source_target_pairs={{0,32},{32,0},{64,96},{96,64},{1,33},{33,1},{65,97},{97,65},{2,34}... | collective-permute-start | bytes 688136 | tf_op jit(solution)/shard_map/ppermute | solution.py:267
  49.8 1.2 %shard_map.48 = (bf16[512,1024]{1,0:T(8,128)(2,1)S(1)}, bf16[512,1024]{1,0:T(8,128)(2,1)S(1)}, f32[1,1024]{1,0:T(1,128)S(1)}) custom-call(s32[1]{0:T(128)} %bitcast.win_ref), custom_call_target="tpu_custom_call" | custom-call | tf_op jit(solution)/shard_map/pallas_call | solution.py:253
  51.0 0.0 collective-permute-done.b
  51.0 1.3 %shard_map.49 = bf16[2,32,6,32,128]{4,3,2,1,0:T(8,128)(2,1)S(1)} custom-call(bf16[7,128,128]{2,1,0:T(8,128)(2,1)S(1)} %get-tuple-element.18.a, bf16[7,128,128]{2,1,0:T(8,128)(2,1)S(1)} %collective-permute-done.b), custom_call_target="tpu_custom_call" | custom-call | tf_op jit(solution)/shard_map/pallas_call | solution.py:134
  52.3 45.6 %all_to_all.11.own_ref = bf16[64,6,32,128]{3,2,1,0:T(8,128)(2,1)S(1)} all-to-all(bf16[64,6,32,128]{3,2,1,0:T(8,128)(2,1)S(1)} %bitcast.4), channel_id=1, replica_groups={{0,1,2,3,4,5,6,7,8,9,10,11,12,13,14,15,16,17,18,19,20,21,22,23,24,25,26..., dimensions={0} | all-to-all | bytes 6291456 | tf_op jit(solution)/shard_map/all_to_all | solution.py:277
  97.9 1.8 %collective-permute-start.1 = (bf16[64,6,32,128]{3,2,1,0:T(8,128)(2,1)S(1)}, bf16[64,6,32,128]{3,2,1,0:T(8,128)(2,1)S(1)}, u32[]{:S(2)}, u32[]{:S(2)}) collective-permute-start(bf16[64,6,32,128]{3,2,1,0:T(8,128)(2,1)S(1)} %all_to_all.11.own_ref), channel_id=1, source_target_pairs={{0,32},{32,0},{64,96},{96,64},{1,33},{33,1},{65,97},{97,65},{2,34}... | collective-permute-start | bytes 9437192 | tf_op jit(solution)/shard_map/ppermute | solution.py:272
  99.7 4.8 %shard_map.50.part_ref = f32[6,512,1024]{2,1,0:T(8,128)S(1)} custom-call(bf16[64,6,32,128]{3,2,1,0:T(8,128)(2,1)S(1)} %all_to_all.11.own_ref, bf16[512,1024]{1,0:T(8,128)(2,1)S(1)} %get-tuple-element.20.table_ref), custom_call_target="tpu_custom_call" | custom-call | flops 6000000000 | bytes 16000000 | tf_op jit(solution)/shard_map/pallas_call | solution.py:163
  104.5 0.4 collective-permute-done.1.far_ref
  104.9 7.1 %shard_map.51 = bf16[6,128,4,1024]{3,2,1,0:T(4,128)(2,1)} custom-call(f32[6,512,1024]{2,1,0:T(8,128)S(1)} %shard_map.50.part_ref, bf16[64,6,32,128]{3,2,1,0:T(8,128)(2,1)S(1)} %collective-permute-done.1.far_ref, bf16[512,1024]{1,0:T(8,128)(2,1)S(1)} %get-tuple-element.21.table_ref, f32[1,1024]{1,0:T(1,128)S(1)} %get-tuple-element.22.taper_ref), custom_call_target="tpu_custom_call" | custom-call | flops 6000000000 | bytes 22000000 | tf_op jit(solution)/shard_map/pallas_call | solution.py:204
Async XLA Ops:
  3.0 43.3 %copy-start = (s32[6]{0:T(128)S(1)}, s32[6]{0:T(128)}, u32[]{:S(2)}) copy-start(s32[6]{0:T(128)} %plan.1) | copy-start | bytes 76
  47.8 3.2 %collective-permute-start = (bf16[7,128,128]{2,1,0:T(8,128)(2,1)S(1)}, bf16[7,128,128]{2,1,0:T(8,128)(2,1)S(1)}, u32[]{:S(2)}, u32[]{:S(2)}) collective-permute-start(bf16[7,128,128]{2,1,0:T(8,128)(2,1)S(1)} %get-tuple-element.19), channel_id=1, source_target_pairs={{0,32},{32,0},{64,96},{96,64},{1,33},{33,1},{65,97},{97,65},{2,34}... | collective-permute-start | bytes 688136 | tf_op jit(solution)/shard_map/ppermute | solution.py:267
  97.9 7.0 %collective-permute-start.1 = (bf16[64,6,32,128]{3,2,1,0:T(8,128)(2,1)S(1)}, bf16[64,6,32,128]{3,2,1,0:T(8,128)(2,1)S(1)}, u32[]{:S(2)}, u32[]{:S(2)}) collective-permute-start(bf16[64,6,32,128]{3,2,1,0:T(8,128)(2,1)S(1)} %all_to_all.11.own_ref), channel_id=1, source_target_pairs={{0,32},{32,0},{64,96},{96,64},{1,33},{33,1},{65,97},{97,65},{2,34}... | collective-permute-start | bytes 9437192 | tf_op jit(solution)/shard_map/ppermute | solution.py:272

commit v4 on v3

v4 whole, which is shorter than its diff:
```python
import math

import jax
import jax.numpy as jnp
from jax import lax
from jax.experimental import pallas as pl
from jax.experimental.pallas import tpu as pltpu
from jax.sharding import PartitionSpec as P

LAGS = 4096
STEPS = 6
FREQ = 512
SRC = 128
HOLDERS = 32
PEERS = 64
LOCAL_WIN = 8
FINE = 4
ROWS = 72
GROUPS = 4
F32 = jnp.float32
BF16 = jnp.bfloat16
CORE_SWAP = [(0, 1), (1, 0), (2, 3), (3, 2)]
SAME_CORE = [[(2 * half + core) * HOLDERS + c for half in range(2) for c in range(HOLDERS)] for core in range(2)]


def params(mebibytes):
    return pltpu.CompilerParams(vmem_limit_bytes=mebibytes * 1024 * 1024)


def pack_kernel(mask_ref, re_ref, im_ref, rec_re_ref, rec_im_ref, out_ref, block):
    lane = lax.broadcasted_iota(jnp.int32, (1, 128), 1)
    usable = jnp.zeros((1, 128), F32)
    for w in range(LOCAL_WIN):
        for r in range(4):
            usable = jnp.where(lane % 32 == 4 * w + r, mask_ref[r, w].astype(F32), usable)
    block[64:, :] = jnp.zeros((64, 128), F32)
    low = lax.broadcasted_iota(jnp.int32, (128, 128), 0) % 8 < 4

    def up(tiles):
        return pltpu.roll(tiles.reshape(128, 128), 124, 0)

    def down(tiles):
        return pltpu.roll(tiles.reshape(128, 128), 4, 0)

    for b in range(2):
        lanes = slice(128 * b, 128 * b + 128)
        for part, ref in enumerate((rec_re_ref, rec_im_ref)):
            for w in range(LOCAL_WIN):
                row = 32 * part + 4 * w
                block[row : row + 4, :] = ref[w, :, lanes].astype(F32)
        turned = block[...].T * usable
        for core, tiles in enumerate((turned, up(turned))):
            out_ref[32 * core + 16 * b : 32 * core + 16 * b + 16, 64:, :] = tiles.reshape(16, 8, 128).astype(BF16)
        for part, ref in enumerate((re_ref, im_ref)):
            for w in range(0, LOCAL_WIN, 4):
                first, second, third, fourth = (ref[w + k, :, lanes].astype(F32).T for k in range(4))
                cores = (
                    (jnp.where(low, first, down(second)), jnp.where(low, third, down(fourth))),
                    (jnp.where(low, up(first), second), jnp.where(low, up(third), fourth)),
                )
                row = 32 * part + 4 * w
                for core, pair in enumerate(cores):
                    both = jnp.concatenate([tiles.reshape(16, 8, 128) for tiles in pair], axis=1)
                    out_ref[32 * core + 16 * b : 32 * core + 16 * b + 16, row : row + 16, :] = both.astype(BF16)


def pack(source_spectra, receiver_spectra, quality_mask):
    return pl.pallas_call(
        pack_kernel,
        grid=(2,),
        in_specs=[
            pl.BlockSpec(memory_space=pltpu.SMEM),
            pl.BlockSpec((LOCAL_WIN, SRC, 256), lambda b: (0, 0, b)),
            pl.BlockSpec((LOCAL_WIN, SRC, 256), lambda b: (0, 0, b + 2)),
            pl.BlockSpec((LOCAL_WIN, 4, 256), lambda b: (0, 0, b)),
            pl.BlockSpec((LOCAL_WIN, 4, 256), lambda b: (0, 0, b + 2)),
        ],
        out_specs=pl.BlockSpec((64, ROWS, 128), lambda b: (b, 0, 0)),
        out_shape=jax.ShapeDtypeStruct((GROUPS * HOLDERS, ROWS, 128), BF16),
        scratch_shapes=[pltpu.VMEM((128, 128), F32)],
        compiler_params=params(60),
    )(quality_mask.T, source_spectra, source_spectra, receiver_spectra, receiver_spectra)


def stack_kernel(plan, held_ref, out_ref, spread, chosen, weights, tall):
    flat = held_ref[:, :, 64:, :].reshape(GROUPS * HOLDERS * 8, 128)
    row = lax.broadcasted_iota(jnp.int32, (128, 128), 0)
    lane = lax.broadcasted_iota(jnp.int32, (128, 128), 1)
    holder = lax.broadcasted_iota(jnp.int32, (HOLDERS, 8, 128), 0)
    here = lax.broadcasted_iota(jnp.int32, (HOLDERS, 8, 128), 2) // 4 == holder
    for k in range(2 * LOCAL_WIN):
        place = jnp.where(row == 4 * k + lane % 4, 1.0, 0.0).astype(BF16)
        tiled = jnp.dot(flat, place, preferred_element_type=F32).reshape(GROUPS, HOLDERS, 8, 128)
        for group in range(GROUPS):
            one = jnp.sum(jnp.where(here, tiled[group], 0.0), axis=0)
            spread[group, pl.ds(k, FINE, stride=16), :] = one[:FINE]
    for i in range(FINE):
        real, imag = [], []
        for group in range(GROUPS):
            tile = spread[group, 16 * i : 16 * i + 16, :]
            real += [tile]
            imag += [-tile[8:], tile[:8]]
        both = jnp.concatenate([jnp.concatenate(real, axis=0), jnp.concatenate(imag, axis=0)], axis=1)
        weights[i] = both.T.astype(BF16)

    @pl.loop(0, STEPS, step=2)
    def _(step):
        for k in range(2):
            for group in range(GROUPS):
                chosen[k, group] = held_ref[group, plan[step + k], :64, :].astype(F32)
        for i in range(FINE):
            pair = [
                jnp.concatenate([chosen[k, group, pl.ds(i, 16, stride=FINE), :] for group in range(GROUPS)], axis=0)
                for k in range(2)
            ]
            block = jnp.concatenate(pair, axis=1).astype(BF16)
            both = jnp.dot(weights[i], block, preferred_element_type=F32)
            for k in range(2):
                tall[k, pl.ds(i, 128, stride=8), :] = both[:128, 128 * k : 128 * k + 128]
                tall[k, pl.ds(FINE + i, 128, stride=8), :] = both[128:, 128 * k : 128 * k + 128]
        for k in range(2):
            spectra = tall[k].reshape(HOLDERS, 32, 128).astype(BF16)
            for half in range(2):
                out_ref[half, :, step + k] = spectra


def stack(plan, held):
    return pl.pallas_call(
        stack_kernel,
        in_specs=[pl.BlockSpec(memory_space=pltpu.SMEM), pl.BlockSpec(memory_space=pltpu.VMEM)],
        out_shape=jax.ShapeDtypeStruct((2, HOLDERS, STEPS, 32, 128), BF16),
        scratch_shapes=[
            pltpu.VMEM((GROUPS, 64, 128), F32),
            pltpu.VMEM((2, GROUPS, 64, 128), F32),
            pltpu.VMEM((FINE, 256, 64), BF16),
            pltpu.VMEM((2, 1024, 128), F32),
        ],
        compiler_params=params(8),
    )(plan, held).reshape(PEERS, STEPS, 32, 128)


def arrange(ref, step, lhs):
    held = ref[:, step].astype(F32)
    for r in range(4):
        turned = held[:, 8 * r : 8 * r + 8, :].reshape(512, 128).T
        for b in range(4):
            lhs[b, pl.ds(r, 128, stride=4), :] = turned[:, 128 * b : 128 * b + 128]


def rows(lhs):
    return jnp.concatenate([lhs[b].astype(BF16) for b in range(4)], axis=1)


def fill_tables(own_ref, far_ref, taper_ref):
    count = taper_ref.shape[1]
    scale = 1.0 / math.sqrt(FREQ * LOCAL_WIN * GROUPS)
    start = lax.axis_index("win") * count
    core = lax.axis_index("win") % 2
    shift = lax.broadcasted_iota(jnp.int32, (8, count), 1) + (start - LAGS // 2)
    index = lax.broadcasted_iota(jnp.int32, (8, count), 0)

    def waves(wave):
        angle = ((wave * shift) & (2 * LAGS - 1)).astype(F32) * (math.pi / LAGS)
        return jnp.cos(angle), jnp.sin(angle)

    high_cos, high_sin = waves(64 * index + 64)
    mid_cos, mid_sin = waves(8 * index)
    low_cos, low_sin = waves(index)
    high_cos, high_sin = high_cos * scale, high_sin * scale
    for ref, h in ((own_ref, core), (far_ref, 1 - core)):
        def rows(wave):
            return jnp.where(h == 0, jnp.concatenate([wave[:4]] * 2, axis=0), jnp.concatenate([wave[4:]] * 2, axis=0))

        fine_cos, fine_sin = rows(low_cos), rows(low_sin)
        real = index < 4
        by_cos = jnp.where(real, fine_cos, -fine_sin)
        by_sin = jnp.where(real, -fine_sin, -fine_cos)
        for a in range(8):
            for b in range(8):
                cos = high_cos[a : a + 1] * mid_cos[b : b + 1] - high_sin[a : a + 1] * mid_sin[b : b + 1]
                sin = high_sin[a : a + 1] * mid_cos[b : b + 1] + high_cos[a : a + 1] * mid_sin[b : b + 1]
                ref[8 * (8 * a + b) : 8 * (8 * a + b) + 8, :] = (cos * by_cos + sin * by_sin).astype(BF16)
    position = lax.broadcasted_iota(jnp.int32, (1, count), 1) + start
    edge = jnp.minimum(position, LAGS - 1 - position) + 1
    taper_ref[...] = jnp.minimum(1.0, edge.astype(F32) / (LAGS // 16))


def begin_kernel(own_ref, out_ref, far_table, taper_ref, own_table, lhs):
    fill_tables(own_table, far_table, taper_ref)

    @pl.loop(0, STEPS)
    def _(step):
        arrange(own_ref, step, lhs)
        out_ref[step] = jnp.dot(rows(lhs), own_table[...], preferred_element_type=F32)


def begin(own, count):
    return pl.pallas_call(
        begin_kernel,
        out_shape=[
            jax.ShapeDtypeStruct((STEPS, 512, count), F32),
            jax.ShapeDtypeStruct((512, count), BF16),
            jax.ShapeDtypeStruct((1, count), F32),
        ],
        scratch_shapes=[pltpu.VMEM((512, count), BF16), pltpu.VMEM((4, 512, 128), F32)],
        compiler_params=params(8),
        cost_estimate=pl.CostEstimate(flops=STEPS * 1_000_000_000, bytes_accessed=16_000_000, transcendentals=0),
    )(own)


def finish_kernel(part_ref, far_ref, table_ref, taper_ref, out_ref, even, odd, ready, sems):
    count = table_ref.shape[1]
    lhs = (even, odd)

    def send(step, piece):
        sources = pl.ds(64 * piece, 64)
        return pltpu.make_async_copy(ready.at[step, sources], out_ref.at[step, sources], sems.at[step, piece])

    arrange(far_ref, 0, even)
    for step in range(STEPS):
        block = rows(lhs[step % 2])
        for piece in range(2):
            here = slice(256 * piece, 256 * piece + 256)
            for n in range(0, count, 256):
                lags = slice(n, n + 256)
                total = jnp.dot(block[here], table_ref[:, lags], preferred_element_type=F32)
                total = (total + part_ref[step, here, lags]) * taper_ref[:, lags]
                ready[step, 64 * piece : 64 * piece + 64, :, lags] = total.reshape(64, 4, 256).astype(BF16)
            send(step, piece).start()
        if step + 1 < STEPS:
            arrange(far_ref, step + 1, lhs[1 - step % 2])
    for step in range(STEPS):
        for piece in range(2):
            send(step, piece).wait()


def finish(part, far, table, taper):
    count = table.shape[1]
    return pl.pallas_call(
        finish_kernel,
        out_specs=pl.BlockSpec(memory_space=pl.ANY),
        out_shape=jax.ShapeDtypeStruct((STEPS, SRC, 4, count), BF16),
        scratch_shapes=[
            pltpu.VMEM((4, 512, 128), F32),
            pltpu.VMEM((4, 512, 128), F32),
            pltpu.VMEM((STEPS, SRC, 4, count), BF16),
            pltpu.SemaphoreType.DMA((STEPS, 2)),
        ],
        compiler_params=params(24),
        cost_estimate=pl.CostEstimate(flops=STEPS * 1_000_000_000, bytes_accessed=22_000_000, transcendentals=0),
    )(part, far, table, taper)


def shards(source_spectra, receiver_spectra, quality_mask, owner_plan):
    packed = pack(source_spectra, receiver_spectra, quality_mask)
    held = lax.all_to_all(packed, ("win", "chan"), 0, 0, tiled=True).reshape(GROUPS, HOLDERS, ROWS, 128)
    own = lax.all_to_all(
        stack(owner_plan, held), ("win", "chan"), 0, 0, tiled=True, axis_index_groups=SAME_CORE
    )
    far = lax.ppermute(own, "win", CORE_SWAP)
    part, far_table, taper = begin(own, LAGS // GROUPS)
    return finish(part, far, far_table, taper)


def solution(mesh):
    return jax.shard_map(
        shards,
        mesh=mesh,
        in_specs=(P("win", "chan", None), P("win", "chan", None), P("win", "chan"), P()),
        out_specs=P(None, None, "chan", "win"),
        check_vma=False,
    )
```

time: 112 us -> 110 us (0.982)
  starting transfers between devices: 3.76 us -> 2.16 us
    ppermute x1 -> x0, starting transfers between devices: 2.01 us -> none  [shards(): from_core = lax.ppermute(other, 'win', CORE_SWAP)]
    pallas_call x1, Pallas kernels: 7.11 us -> 5.66 us  [finish(): pl.pallas_call(finish_kernel, out_specs=pl.BlockSpec(memory_space=pl.ANY)...]
    pallas_call x4 -> x2, Pallas kernels: 8.86 us -> 9.28 us  [the longest x1 6.11 us: begin(): pl.pallas_call(begin_kernel, out_shape=[jax.ShapeDtypeStruct((STEPS, 512,...]
  transfers between devices with their start and end apart: 2 -> 1, of which waited for: 1 -> 0; matrix products, arithmetic and copies ran while one was open for 0% -> 0% of each run, Pallas kernels for 5% -> 6%
where the time goes in v4:
time: 110 us; the launch traced here: 109 us
  blocking collectives  88.9 us (81%)
  Pallas kernels  18.3 us (17%)
  starting transfers between devices  2.16 us (2%)
    all_to_all x1, blocking collectives, shards(): lax.all_to_all(stack(owner_plan, held), ('win', 'chan'), 0, 0, tiled=True...  44.6 us
    all_to_all x1, blocking collectives, shards(): lax.all_to_all(packed, ('win', 'chan'), 0, 0, tiled=True)  44.3 us
    pallas_call x1, Pallas kernels, begin(): pl.pallas_call(begin_kernel, out_shape=[jax.ShapeDtypeStruct((STEPS, 512,...  6.11 us
    pallas_call x1, Pallas kernels, finish(): pl.pallas_call(finish_kernel, out_specs=pl.BlockSpec(memory_space=pl.ANY)...  5.66 us
    pallas_call x1, Pallas kernels, pack(): pl.pallas_call(pack_kernel, grid=(2,), in_specs=[pl.BlockSpec(memory_spac...  3.32 us
    pallas_call x1, Pallas kernels, stack(): pl.pallas_call(stack_kernel, in_specs=[pl.BlockSpec(memory_space=pltpu.SM...  3.17 us
  transfers between devices with their start and end apart: 1, of which 0 were waited for; matrix products, arithmetic and copies ran while one was open for 0% of the time, Pallas kernels for 6%

profile of v4, /device:TPU:1, one launch (start us, length us, event | category | flops | bytes accessed | tf_op | source)
XLA Modules:
  0.0 109.4 jit_solution(2203914675693028049)
XLA Ops:
  0.0 3.3 %shard_map.46 = bf16[128,72,128]{2,1,0:T(8,128)(2,1)} custom-call(s32[4,8]{1,0:T(4,128)} %bitcast.5, bf16[8,128,1024]{2,1,0:T(8,128)(2,1)} %im_ref.1, bf16[8,128,1024]{2,1,0:T(8,128)(2,1)} %im_ref.1, bf16[8,4,1024]{2,1,0:T(4,128)(2,1)} %rec_im_ref.1, bf16[8,4,1024]{2,1,0:T(4,128)(2,1)} %rec_im_ref.1), custom_call_target="tpu_custom_call" | custom-call | tf_op jit(solution)/shard_map/pallas_call | solution.py:68
  3.3 0.0 copy-start
  3.3 44.3 %all_to_all.10 = bf16[128,72,128]{2,1,0:T(8,128)(2,1)S(1)} all-to-all(bf16[128,72,128]{2,1,0:T(8,128)(2,1)} %shard_map.46), channel_id=1, replica_groups=mesh['win'=4,'chan'=32] {'win','chan'}, dimensions={0} | all-to-all | bytes 4718592 | tf_op jit(solution)/shard_map/all_to_all | solution.py:256
  47.7 0.0 copy-done
  47.7 3.2 %shard_map.47 = bf16[2,32,6,32,128]{4,3,2,1,0:T(8,128)(2,1)S(1)} custom-call(s32[6]{0:T(128)S(1)} %copy-done, bf16[4,32,72,128]{3,2,1,0:T(8,128)(2,1)S(1)} %bitcast.4), custom_call_target="tpu_custom_call" | custom-call | tf_op jit(solution)/shard_map/pallas_call | solution.py:128
  50.8 44.6 %all_to_all.11.own_ref = bf16[64,6,32,128]{3,2,1,0:T(8,128)(2,1)S(1)} all-to-all(bf16[64,6,32,128]{3,2,1,0:T(8,128)(2,1)S(1)} %bitcast.3), channel_id=1, replica_groups={{0,1,2,3,4,5,6,7,8,9,10,11,12,13,14,15,16,17,18,19,20,21,22,23,24,25,26..., dimensions={0} | all-to-all | bytes 6291456 | tf_op jit(solution)/shard_map/all_to_all | solution.py:257
  95.5 2.2 %collective-permute-start = (bf16[64,6,32,128]{3,2,1,0:T(8,128)(2,1)S(1)}, bf16[64,6,32,128]{3,2,1,0:T(8,128)(2,1)S(1)}, u32[]{:S(2)}, u32[]{:S(2)}) collective-permute-start(bf16[64,6,32,128]{3,2,1,0:T(8,128)(2,1)S(1)} %all_to_all.11.own_ref), channel_id=1, source_target_pairs={{0,32},{32,0},{64,96},{96,64},{1,33},{33,1},{65,97},{97,65},{2,34}... | collective-permute-start | bytes 9437192 | tf_op jit(solution)/shard_map/ppermute | solution.py:260
  97.6 6.1 %shard_map.48 = (f32[6,512,1024]{2,1,0:T(8,128)S(1)}, bf16[512,1024]{1,0:T(8,128)(2,1)S(1)}, f32[1,1024]{1,0:T(1,128)S(1)}) custom-call(bf16[64,6,32,128]{3,2,1,0:T(8,128)(2,1)S(1)} %all_to_all.11.own_ref), custom_call_target="tpu_custom_call" | custom-call | flops 6000000000 | bytes 16000000 | tf_op jit(solution)/shard_map/pallas_call | solution.py:198
  103.7 0.0 collective-permute-done.far_ref
  103.7 5.7 %shard_map.49 = bf16[6,128,4,1024]{3,2,1,0:T(4,128)(2,1)} custom-call(f32[6,512,1024]{2,1,0:T(8,128)S(1)} %get-tuple-element.8.part_ref, bf16[64,6,32,128]{3,2,1,0:T(8,128)(2,1)S(1)} %collective-permute-done.far_ref, bf16[512,1024]{1,0:T(8,128)(2,1)S(1)} %get-tuple-element.9.table_ref, f32[1,1024]{1,0:T(1,128)S(1)} %get-tuple-element.10.taper_ref), custom_call_target="tpu_custom_call" | custom-call | flops 6000000000 | bytes 22000000 | tf_op jit(solution)/shard_map/pallas_call | solution.py:239
Async XLA Ops:
  3.3 44.3 %copy-start = (s32[6]{0:T(128)S(1)}, s32[6]{0:T(128)}, u32[]{:S(2)}) copy-start(s32[6]{0:T(128)} %plan.1) | copy-start | bytes 76
  95.5 8.3 %collective-permute-start = (bf16[64,6,32,128]{3,2,1,0:T(8,128)(2,1)S(1)}, bf16[64,6,32,128]{3,2,1,0:T(8,128)(2,1)S(1)}, u32[]{:S(2)}, u32[]{:S(2)}) collective-permute-start(bf16[64,6,32,128]{3,2,1,0:T(8,128)(2,1)S(1)} %all_to_all.11.own_ref), channel_id=1, source_target_pairs={{0,32},{32,0},{64,96},{96,64},{1,33},{33,1},{65,97},{97,65},{2,34}... | collective-permute-start | bytes 9437192 | tf_op jit(solution)/shard_map/ppermute | solution.py:260

commit v5 on v4

v5 whole, which is shorter than its diff:
```python
import math

import jax
import jax.numpy as jnp
from jax import lax
from jax.experimental import pallas as pl
from jax.experimental.pallas import tpu as pltpu
from jax.sharding import PartitionSpec as P

LAGS = 4096
STEPS = 6
FREQ = 512
SRC = 128
HOLDERS = 32
BLOCKS = 2 * FREQ // 128
SHARE = 3
LOCAL_WIN = 8
FINE = 4
ROWS = 72
GROUPS = 4
F32 = jnp.float32
BF16 = jnp.bfloat16
CORE_SWAP = [(0, 1), (1, 0), (2, 3), (3, 2)]


def params(mebibytes):
    return pltpu.CompilerParams(vmem_limit_bytes=mebibytes * 1024 * 1024)


def pack_kernel(mask_ref, re_ref, im_ref, rec_re_ref, rec_im_ref, out_ref, block):
    lane = lax.broadcasted_iota(jnp.int32, (1, 128), 1)
    usable = jnp.zeros((1, 128), F32)
    for w in range(LOCAL_WIN):
        for r in range(4):
            usable = jnp.where(lane == 4 * w + r, mask_ref[r, w].astype(F32), usable)
    block[:, 32:, :] = jnp.zeros((2, 96, 128), F32)
    low = lax.broadcasted_iota(jnp.int32, (128, 128), 0) % 8 < 4

    def split(first, second):
        down = pltpu.roll(second, 4, 0)
        up = pltpu.roll(first, 124, 0)
        return jnp.where(low, first, down), jnp.where(low, up, second)

    for b in range(2):
        lanes = slice(128 * b, 128 * b + 128)
        for part, ref in enumerate((rec_re_ref, rec_im_ref)):
            for w in range(LOCAL_WIN):
                block[part, 4 * w : 4 * w + 4, :] = ref[w, :, lanes].astype(F32)
        for core, tiles in enumerate(split(block[0].T * usable, block[1].T * usable)):
            out_ref[32 * core + 16 * b : 32 * core + 16 * b + 16, 64:, :] = tiles.reshape(16, 8, 128).astype(BF16)
        for part, ref in enumerate((re_ref, im_ref)):
            for w in range(0, LOCAL_WIN, 4):
                turned = [ref[w + k, :, lanes].astype(F32).T for k in range(4)]
                cores = zip(split(turned[0], turned[1]), split(turned[2], turned[3]))
                row = 32 * part + 4 * w
                for core, pair in enumerate(cores):
                    both = jnp.concatenate([tiles.reshape(16, 8, 128) for tiles in pair], axis=1)
                    out_ref[32 * core + 16 * b : 32 * core + 16 * b + 16, row : row + 16, :] = both.astype(BF16)


def pack(source_spectra, receiver_spectra, quality_mask):
    return pl.pallas_call(
        pack_kernel,
        grid=(2,),
        in_specs=[
            pl.BlockSpec(memory_space=pltpu.SMEM),
            pl.BlockSpec((LOCAL_WIN, SRC, 256), lambda b: (0, 0, b)),
            pl.BlockSpec((LOCAL_WIN, SRC, 256), lambda b: (0, 0, b + 2)),
            pl.BlockSpec((LOCAL_WIN, 4, 256), lambda b: (0, 0, b)),
            pl.BlockSpec((LOCAL_WIN, 4, 256), lambda b: (0, 0, b + 2)),
        ],
        out_specs=pl.BlockSpec((64, ROWS, 128), lambda b: (b, 0, 0)),
        out_shape=jax.ShapeDtypeStruct((GROUPS * HOLDERS, ROWS, 128), BF16),
        scratch_shapes=[pltpu.VMEM((2, 128, 128), F32)],
        compiler_params=params(60),
    )(quality_mask.T, source_spectra, source_spectra, receiver_spectra, receiver_spectra)


def stack_kernel(plan, held_ref, out_ref, spread, chosen, weights, tall):
    flat = held_ref[:, :, 64:, :].reshape(GROUPS * HOLDERS * 8, 128)
    row = lax.broadcasted_iota(jnp.int32, (128, 256), 0)
    lane = lax.broadcasted_iota(jnp.int32, (128, 256), 1)
    holder = lax.broadcasted_iota(jnp.int32, (HOLDERS, 8, 256), 0)
    here = lax.broadcasted_iota(jnp.int32, (HOLDERS, 8, 256), 2) % 128 // 4 == holder
    for w in range(0, LOCAL_WIN, 2):
        place = jnp.where(row == 4 * (w + lane // 128) + lane % 4, 1.0, 0.0).astype(BF16)
        tiled = jnp.dot(flat, place, preferred_element_type=F32).reshape(GROUPS, HOLDERS, 8, 256)
        for group in range(GROUPS):
            two = jnp.sum(jnp.where(here, tiled[group], 0.0), axis=0)
            for k in range(2):
                for part in range(2):
                    one = two[FINE * part : FINE * part + FINE, 128 * k : 128 * k + 128]
                    spread[group, pl.ds(LOCAL_WIN * part + w + k, FINE, stride=16), :] = one
    for i in range(FINE):
        real, imag = [], []
        for group in range(GROUPS):
            tile = spread[group, 16 * i : 16 * i + 16, :]
            real += [tile]
            imag += [-tile[8:], tile[:8]]
        both = jnp.concatenate([jnp.concatenate(real, axis=0), jnp.concatenate(imag, axis=0)], axis=1)
        weights[i] = both.T.astype(BF16)

    @pl.loop(0, STEPS, step=2)
    def _(step):
        for k in range(2):
            for group in range(GROUPS):
                chosen[k, group] = held_ref[group, plan[step + k], :64, :].astype(F32)
        for i in range(FINE):
            pair = [
                jnp.concatenate([chosen[k, group, pl.ds(i, 16, stride=FINE), :] for group in range(GROUPS)], axis=0)
                for k in range(2)
            ]
            block = jnp.concatenate(pair, axis=1).astype(BF16)
            both = jnp.dot(weights[i], block, preferred_element_type=F32)
            for k in range(2):
                tall[k, pl.ds(i, 128, stride=8), :] = both[:128, 128 * k : 128 * k + 128]
                tall[k, pl.ds(FINE + i, 128, stride=8), :] = both[128:, 128 * k : 128 * k + 128]
        for k in range(2):
            spectra = tall[k].reshape(HOLDERS, 32, 128).astype(BF16)
            for half in range(2):
                out_ref[2 * half + (step + k) // SHARE, :, lax.rem(step + k, SHARE)] = spectra


def stack(plan, held):
    return pl.pallas_call(
        stack_kernel,
        in_specs=[pl.BlockSpec(memory_space=pltpu.SMEM), pl.BlockSpec(memory_space=pltpu.VMEM)],
        out_shape=jax.ShapeDtypeStruct((GROUPS, HOLDERS, SHARE, 32, 128), BF16),
        scratch_shapes=[
            pltpu.VMEM((GROUPS, 64, 128), F32),
            pltpu.VMEM((2, GROUPS, 64, 128), F32),
            pltpu.VMEM((FINE, 256, 64), BF16),
            pltpu.VMEM((2, 1024, 128), F32),
        ],
        compiler_params=params(8),
    )(plan, held).reshape(GROUPS * HOLDERS, SHARE, 32, 128)


def arrange(ref, step, lhs):
    held = ref[:, step].astype(F32)
    for r in range(4):
        turned = held[:, 8 * r : 8 * r + 8, :].reshape(2 * FREQ, 128).T
        for b in range(BLOCKS):
            lhs[b, pl.ds(r, 128, stride=4), :] = turned[:, 128 * b : 128 * b + 128]


def rows(lhs):
    return jnp.concatenate([lhs[b].astype(BF16) for b in range(BLOCKS)], axis=1)


def fill_table(table_ref, taper_ref):
    count = taper_ref.shape[1]
    scale = 1.0 / math.sqrt(FREQ * LOCAL_WIN * GROUPS)
    start = lax.axis_index("win") * count
    shift = lax.broadcasted_iota(jnp.int32, (8, count), 1) + (start - LAGS // 2)
    index = lax.broadcasted_iota(jnp.int32, (8, count), 0)

    def waves(wave):
        angle = ((wave * shift) & (2 * LAGS - 1)).astype(F32) * (math.pi / LAGS)
        return jnp.cos(angle), jnp.sin(angle)

    high_cos, high_sin = waves(64 * index + 64)
    mid_cos, mid_sin = waves(8 * index)
    low_cos, low_sin = waves(index)
    high_cos, high_sin = high_cos * scale, high_sin * scale
    real = index < 4
    fine = []
    for h in range(2):
        cos = jnp.concatenate([low_cos[4 * h : 4 * h + 4]] * 2, axis=0)
        sin = jnp.concatenate([low_sin[4 * h : 4 * h + 4]] * 2, axis=0)
        fine.append((jnp.where(real, cos, -sin), jnp.where(real, -sin, -cos)))
    for a in range(8):
        for b in range(8):
            cos = high_cos[a : a + 1] * mid_cos[b : b + 1] - high_sin[a : a + 1] * mid_sin[b : b + 1]
            sin = high_sin[a : a + 1] * mid_cos[b : b + 1] + high_cos[a : a + 1] * mid_sin[b : b + 1]
            for h, (by_cos, by_sin) in enumerate(fine):
                row = 8 * ((2 * (a // 4) + h) * HOLDERS + 8 * (a % 4) + b)
                table_ref[row : row + 8, :] = (cos * by_cos + sin * by_sin).astype(BF16)
    position = lax.broadcasted_iota(jnp.int32, (1, count), 1) + start
    edge = jnp.minimum(position, LAGS - 1 - position) + 1
    taper_ref[...] = jnp.minimum(1.0, edge.astype(F32) / (LAGS // 16))


def project(held_ref, table_ref, taper_ref, out_ref, first, even, odd, ready, sems):
    count = table_ref.shape[1]
    lhs = (even, odd)

    def send(step, piece):
        sources = pl.ds(64 * piece, 64)
        return pltpu.make_async_copy(ready.at[step, sources], out_ref.at[first + step, sources], sems.at[step, piece])

    arrange(held_ref, 0, even)
    for step in range(SHARE):
        block = rows(lhs[step % 2])
        for piece in range(2):
            here = slice(256 * piece, 256 * piece + 256)
            for n in range(0, count, 256):
                lags = slice(n, n + 256)
                total = jnp.dot(block[here], table_ref[:, lags], preferred_element_type=F32) * taper_ref[:, lags]
                ready[step, 64 * piece : 64 * piece + 64, :, lags] = total.reshape(64, 4, 256).astype(BF16)
            send(step, piece).start()
        if step + 1 < SHARE:
            arrange(held_ref, step + 1, lhs[1 - step % 2])
    for step in range(SHARE):
        for piece in range(2):
            send(step, piece).wait()


def begin_kernel(own_ref, out_ref, table_ref, taper_ref, *scratch):
    fill_table(table_ref, taper_ref)
    project(own_ref, table_ref, taper_ref, out_ref, SHARE * (lax.axis_index("win") % 2), *scratch)


def finish_kernel(far_ref, table_ref, taper_ref, _, out_ref, *scratch):
    project(far_ref, table_ref, taper_ref, out_ref, SHARE * (1 - lax.axis_index("win") % 2), *scratch)


def settings(count):
    return dict(
        scratch_shapes=[
            pltpu.VMEM((BLOCKS, 512, 128), F32),
            pltpu.VMEM((BLOCKS, 512, 128), F32),
            pltpu.VMEM((SHARE, SRC, 4, count), BF16),
            pltpu.SemaphoreType.DMA((SHARE, 2)),
        ],
        compiler_params=params(16),
        cost_estimate=pl.CostEstimate(flops=SHARE * 2_000_000_000, bytes_accessed=10_000_000, transcendentals=0),
    )


def begin(own, count):
    return pl.pallas_call(
        begin_kernel,
        out_specs=[pl.BlockSpec(memory_space=pl.ANY)] + [pl.BlockSpec(memory_space=pltpu.VMEM)] * 2,
        out_shape=[
            jax.ShapeDtypeStruct((STEPS, SRC, 4, count), BF16),
            jax.ShapeDtypeStruct((2 * FREQ, count), BF16),
            jax.ShapeDtypeStruct((1, count), F32),
        ],
        **settings(count),
    )(own)


def finish(far, table, taper, out):
    vmem = pl.BlockSpec(memory_space=pltpu.VMEM)
    return pl.pallas_call(
        finish_kernel,
        in_specs=[vmem, vmem, vmem, pl.BlockSpec(memory_space=pl.ANY)],
        out_specs=pl.BlockSpec(memory_space=pl.ANY),
        out_shape=jax.ShapeDtypeStruct(out.shape, BF16),
        input_output_aliases={3: 0},
        **settings(table.shape[1]),
    )(far, table, taper, out)


def exchange(blocks):
    return lax.all_to_all(blocks, ("win", "chan"), 0, 0, tiled=True)


def shards(source_spectra, receiver_spectra, quality_mask, owner_plan):
    packed = pack(source_spectra, receiver_spectra, quality_mask)
    held = exchange(packed).reshape(GROUPS, HOLDERS, ROWS, 128)
    own = exchange(stack(owner_plan, held))
    far = lax.ppermute(own, "win", CORE_SWAP)
    out, table, taper = begin(own, LAGS // GROUPS)
    return finish(far, table, taper, out)


def solution(mesh):
    return jax.shard_map(
        shards,
        mesh=mesh,
        in_specs=(P("win", "chan", None), P("win", "chan", None), P("win", "chan"), P()),
        out_specs=P(None, None, "chan", "win"),
        check_vma=False,
    )
```

time: 110 us -> 108 us (0.982)
  Pallas kernels: 18.3 us -> 16.4 us
  blocking collectives: 88.9 us -> 90.2 us
    pallas_call x2, Pallas kernels: 11.8 us -> 10.3 us  [the longest x1 5.71 us: begin(): pl.pallas_call(begin_kernel, out_specs=[pl.BlockSpec(memory_space=pl.ANY)...]
    all_to_all x2, blocking collectives: 88.9 us -> 90.2 us  [exchange(): return lax.all_to_all(blocks, ('win', 'chan'), 0, 0, tiled=True)]
  transfers between devices with their start and end apart: 1 -> 1, of which waited for: 0 -> 0; matrix products, arithmetic and copies ran while one was open for 0% -> 0% of each run, Pallas kernels for 6% -> 5%
where the time goes in v5:
time: 108 us
  blocking collectives  90.2 us (84%)
  Pallas kernels  16.4 us (15%)
  starting transfers between devices  1.14 us (1%)
    all_to_all x2, blocking collectives, exchange(): return lax.all_to_all(blocks, ('win', 'chan'), 0, 0, tiled=True)  90.2 us
    pallas_call x1, Pallas kernels, begin(): pl.pallas_call(begin_kernel, out_specs=[pl.BlockSpec(memory_space=pl.ANY)...  5.71 us
    pallas_call x1, Pallas kernels, finish(): pl.pallas_call(finish_kernel, in_specs=[vmem, vmem, vmem, pl.BlockSpec(me...  4.63 us
    pallas_call x1, Pallas kernels, pack(): pl.pallas_call(pack_kernel, grid=(2,), in_specs=[pl.BlockSpec(memory_spac...  3.35 us
    pallas_call x1, Pallas kernels, stack(): pl.pallas_call(stack_kernel, in_specs=[pl.BlockSpec(memory_space=pltpu.SM...  2.71 us
  transfers between devices with their start and end apart: 1, of which 0 were waited for; matrix products, arithmetic and copies ran while one was open for 0% of the time, Pallas kernels for 5%

profile of v5, /device:TPU:1, one launch (start us, length us, event | category | flops | bytes accessed | tf_op | source)
XLA Modules:
  0.0 107.8 jit_solution(14843798842113298320)
XLA Ops:
  0.0 3.4 %shard_map.46 = bf16[128,72,128]{2,1,0:T(8,128)(2,1)} custom-call(s32[4,8]{1,0:T(4,128)} %bitcast.5, bf16[8,128,1024]{2,1,0:T(8,128)(2,1)} %im_ref.1, bf16[8,128,1024]{2,1,0:T(8,128)(2,1)} %im_ref.1, bf16[8,4,1024]{2,1,0:T(4,128)(2,1)} %rec_im_ref.1, bf16[8,4,1024]{2,1,0:T(4,128)(2,1)} %rec_im_ref.1), custom_call_target="tpu_custom_call" | custom-call | tf_op jit(solution)/shard_map/pallas_call | solution.py:62
  3.4 0.0 copy-start
  3.4 44.3 %all_to_all.10 = bf16[128,72,128]{2,1,0:T(8,128)(2,1)S(1)} all-to-all(bf16[128,72,128]{2,1,0:T(8,128)(2,1)} %shard_map.46), channel_id=1, replica_groups=mesh['win'=4,'chan'=32] {'win','chan'}, dimensions={0} | all-to-all | bytes 4718592 | tf_op jit(solution)/shard_map/all_to_all | solution.py:257
  47.7 0.0 copy-done
  47.7 2.7 %shard_map.47 = bf16[4,32,3,32,128]{4,3,2,1,0:T(8,128)(2,1)S(1)} custom-call(s32[6]{0:T(128)S(1)} %copy-done, bf16[4,32,72,128]{3,2,1,0:T(8,128)(2,1)S(1)} %bitcast.4), custom_call_target="tpu_custom_call" | custom-call | tf_op jit(solution)/shard_map/pallas_call | solution.py:125
  50.4 45.9 %all_to_all.11.own_ref = bf16[128,3,32,128]{3,2,1,0:T(8,128)(2,1)S(1)} all-to-all(bf16[128,3,32,128]{3,2,1,0:T(8,128)(2,1)S(1)} %bitcast.3), channel_id=1, replica_groups=mesh['win'=4,'chan'=32] {'win','chan'}, dimensions={0} | all-to-all | bytes 6291456 | tf_op jit(solution)/shard_map/all_to_all | solution.py:257
  96.3 1.1 %collective-permute-start = (bf16[128,3,32,128]{3,2,1,0:T(8,128)(2,1)S(1)}, bf16[128,3,32,128]{3,2,1,0:T(8,128)(2,1)S(1)}, u32[]{:S(2)}, u32[]{:S(2)}) collective-permute-start(bf16[128,3,32,128]{3,2,1,0:T(8,128)(2,1)S(1)} %all_to_all.11.own_ref), channel_id=1, source_target_pairs={{0,32},{32,0},{64,96},{96,64},{1,33},{33,1},{65,97},{97,65},{2,34}... | collective-permute-start | bytes 9437192 | tf_op jit(solution)/shard_map/ppermute | solution.py:264
  97.5 5.7 %shard_map.48 = (bf16[6,128,4,1024]{3,2,1,0:T(4,128)(2,1)}, bf16[1024,1024]{1,0:T(8,128)(2,1)S(1)}, f32[1,1024]{1,0:T(1,128)S(1)}) custom-call(bf16[128,3,32,128]{3,2,1,0:T(8,128)(2,1)S(1)} %all_to_all.11.own_ref), custom_call_target="tpu_custom_call" | custom-call | flops 6000000000 | bytes 10000000 | tf_op jit(solution)/shard_map/pallas_call | solution.py:232
  103.2 0.0 collective-permute-done.far_ref
  103.2 4.6 %shard_map.49 = bf16[6,128,4,1024]{3,2,1,0:T(4,128)(2,1)} custom-call(bf16[128,3,32,128]{3,2,1,0:T(8,128)(2,1)S(1)} %collective-permute-done.far_ref, bf16[1024,1024]{1,0:T(8,128)(2,1)S(1)} %get-tuple-element.8.table_ref, f32[1,1024]{1,0:T(1,128)S(1)} %get-tuple-element.9.taper_ref, ...), custom_call_target="tpu_custom_call", output_to_operand_aliasing={{}: (3, {})} | custom-call | flops 6000000000 | bytes 10000000 | tf_op jit(solution)/shard_map/pallas_call | solution.py:246
Async XLA Ops:
  3.4 44.3 %copy-start = (s32[6]{0:T(128)S(1)}, s32[6]{0:T(128)}, u32[]{:S(2)}) copy-start(s32[6]{0:T(128)} %plan.1) | copy-start | bytes 76
  96.3 6.9 %collective-permute-start = (bf16[128,3,32,128]{3,2,1,0:T(8,128)(2,1)S(1)}, bf16[128,3,32,128]{3,2,1,0:T(8,128)(2,1)S(1)}, u32[]{:S(2)}, u32[]{:S(2)}) collective-permute-start(bf16[128,3,32,128]{3,2,1,0:T(8,128)(2,1)S(1)} %all_to_all.11.own_ref), channel_id=1, source_target_pairs={{0,32},{32,0},{64,96},{96,64},{1,33},{33,1},{65,97},{97,65},{2,34}... | collective-permute-start | bytes 9437192 | tf_op jit(solution)/shard_map/ppermute | solution.py:264

commit v6 on v5

--- a/solution.py
+++ b/solution.py
@@ -70,9 +70,9 @@
             pl.BlockSpec((LOCAL_WIN, 4, 256), lambda b: (0, 0, b + 2)),
         ],
         out_specs=pl.BlockSpec((64, ROWS, 128), lambda b: (b, 0, 0)),
-        out_shape=jax.ShapeDtypeStruct((GROUPS * HOLDERS, ROWS, 128), BF16),
+        out_shape=pltpu.VMEM((GROUPS * HOLDERS, ROWS, 128), BF16),
         scratch_shapes=[pltpu.VMEM((2, 128, 128), F32)],
-        compiler_params=params(60),
+        compiler_params=params(58),
     )(quality_mask.T, source_spectra, source_spectra, receiver_spectra, receiver_spectra)
 
 
@@ -100,8 +100,7 @@
         both = jnp.concatenate([jnp.concatenate(real, axis=0), jnp.concatenate(imag, axis=0)], axis=1)
         weights[i] = both.T.astype(BF16)
 
-    @pl.loop(0, STEPS, step=2)
-    def _(step):
+    for step in range(0, STEPS, 2):
         for k in range(2):
             for group in range(GROUPS):
                 chosen[k, group] = held_ref[group, plan[step + k], :64, :].astype(F32)
@@ -118,7 +117,7 @@
         for k in range(2):
             spectra = tall[k].reshape(HOLDERS, 32, 128).astype(BF16)
             for half in range(2):
-                out_ref[2 * half + (step + k) // SHARE, :, lax.rem(step + k, SHARE)] = spectra
+                out_ref[2 * half + (step + k) // SHARE, :, (step + k) % SHARE] = spectra
 
 
 def stack(plan, held):
@@ -170,12 +169,13 @@
         sin = jnp.concatenate([low_sin[4 * h : 4 * h + 4]] * 2, axis=0)
         fine.append((jnp.where(real, cos, -sin), jnp.where(real, -sin, -cos)))
     for a in range(8):
-        for b in range(8):
-            cos = high_cos[a : a + 1] * mid_cos[b : b + 1] - high_sin[a : a + 1] * mid_sin[b : b + 1]
-            sin = high_sin[a : a + 1] * mid_cos[b : b + 1] + high_cos[a : a + 1] * mid_sin[b : b + 1]
-            for h, (by_cos, by_sin) in enumerate(fine):
+        cos = high_cos[a : a + 1] * mid_cos - high_sin[a : a + 1] * mid_sin
+        sin = high_sin[a : a + 1] * mid_cos + high_cos[a : a + 1] * mid_sin
+        for h, (by_cos, by_sin) in enumerate(fine):
+            for b in range(0, 8, 2):
+                pair = [cos[k : k + 1] * by_cos + sin[k : k + 1] * by_sin for k in (b, b + 1)]
                 row = 8 * ((2 * (a // 4) + h) * HOLDERS + 8 * (a % 4) + b)
-                table_ref[row : row + 8, :] = (cos * by_cos + sin * by_sin).astype(BF16)
+                table_ref[row : row + 16, :] = jnp.concatenate(pair, axis=0).astype(BF16)
     position = lax.broadcasted_iota(jnp.int32, (1, count), 1) + start
     edge = jnp.minimum(position, LAGS - 1 - position) + 1
     taper_ref[...] = jnp.minimum(1.0, edge.astype(F32) / (LAGS // 16))

time: 108 us -> 106 us (0.981)
  Pallas kernels: 16.4 us -> 15 us
where the time goes in v6:
time: 106 us
  blocking collectives  90 us (85%)
  Pallas kernels  15 us (14%)
  starting transfers between devices  1.14 us (1%)
    all_to_all x2, blocking collectives, exchange(): return lax.all_to_all(blocks, ('win', 'chan'), 0, 0, tiled=True)  90 us
    pallas_call x1, Pallas kernels, begin(): pl.pallas_call(begin_kernel, out_specs=[pl.BlockSpec(memory_space=pl.ANY)...  5.72 us
    pallas_call x1, Pallas kernels, finish(): pl.pallas_call(finish_kernel, in_specs=[vmem, vmem, vmem, pl.BlockSpec(me...  4.68 us
    pallas_call x1, Pallas kernels, pack(): pl.pallas_call(pack_kernel, grid=(2,), in_specs=[pl.BlockSpec(memory_spac...  2.36 us
    pallas_call x1, Pallas kernels, stack(): pl.pallas_call(stack_kernel, in_specs=[pl.BlockSpec(memory_space=pltpu.SM...  2.21 us
  transfers between devices with their start and end apart: 1, of which 0 were waited for; matrix products, arithmetic and copies ran while one was open for 0% of the time, Pallas kernels for 5%

profile of v6, /device:TPU:1, one launch (start us, length us, event | category | flops | bytes accessed | tf_op | source)
XLA Modules:
  0.0 106.2 jit_solution(4631077933013643515)
XLA Ops:
  0.0 2.4 %shard_map.46 = bf16[128,72,128]{2,1,0:T(8,128)(2,1)S(1)} custom-call(s32[4,8]{1,0:T(4,128)} %bitcast.5, bf16[8,128,1024]{2,1,0:T(8,128)(2,1)} %im_ref.1, bf16[8,128,1024]{2,1,0:T(8,128)(2,1)} %im_ref.1, bf16[8,4,1024]{2,1,0:T(4,128)(2,1)} %rec_im_ref.1, bf16[8,4,1024]{2,1,0:T(4,128)(2,1)} %rec_im_ref.1), custom_call_target="tpu_custom_call" | custom-call | tf_op jit(solution)/shard_map/pallas_call | solution.py:62
  2.4 0.0 copy-start
  2.4 44.1 %all_to_all.10 = bf16[128,72,128]{2,1,0:T(8,128)(2,1)S(1)} all-to-all(bf16[128,72,128]{2,1,0:T(8,128)(2,1)S(1)} %shard_map.46), channel_id=1, replica_groups=mesh['win'=4,'chan'=32] {'win','chan'}, dimensions={0} | all-to-all | bytes 4718592 | tf_op jit(solution)/shard_map/all_to_all | solution.py:257
  46.5 0.0 copy-done
  46.5 2.2 %shard_map.47 = bf16[4,32,3,32,128]{4,3,2,1,0:T(8,128)(2,1)S(1)} custom-call(s32[6]{0:T(128)S(1)} %copy-done, bf16[4,32,72,128]{3,2,1,0:T(8,128)(2,1)S(1)} %bitcast.4), custom_call_target="tpu_custom_call" | custom-call | tf_op jit(solution)/shard_map/pallas_call | solution.py:124
  48.7 45.9 %all_to_all.11.own_ref = bf16[128,3,32,128]{3,2,1,0:T(8,128)(2,1)S(1)} all-to-all(bf16[128,3,32,128]{3,2,1,0:T(8,128)(2,1)S(1)} %bitcast.3), channel_id=1, replica_groups=mesh['win'=4,'chan'=32] {'win','chan'}, dimensions={0} | all-to-all | bytes 6291456 | tf_op jit(solution)/shard_map/all_to_all | solution.py:257
  94.6 1.1 %collective-permute-start = (bf16[128,3,32,128]{3,2,1,0:T(8,128)(2,1)S(1)}, bf16[128,3,32,128]{3,2,1,0:T(8,128)(2,1)S(1)}, u32[]{:S(2)}, u32[]{:S(2)}) collective-permute-start(bf16[128,3,32,128]{3,2,1,0:T(8,128)(2,1)S(1)} %all_to_all.11.own_ref), channel_id=1, source_target_pairs={{0,32},{32,0},{64,96},{96,64},{1,33},{33,1},{65,97},{97,65},{2,34}... | collective-permute-start | bytes 9437192 | tf_op jit(solution)/shard_map/ppermute | solution.py:264
  95.8 5.7 %shard_map.48 = (bf16[6,128,4,1024]{3,2,1,0:T(4,128)(2,1)}, bf16[1024,1024]{1,0:T(8,128)(2,1)S(1)}, f32[1,1024]{1,0:T(1,128)S(1)}) custom-call(bf16[128,3,32,128]{3,2,1,0:T(8,128)(2,1)S(1)} %all_to_all.11.own_ref), custom_call_target="tpu_custom_call" | custom-call | flops 6000000000 | bytes 10000000 | tf_op jit(solution)/shard_map/pallas_call | solution.py:232
  101.5 0.0 collective-permute-done.far_ref
  101.5 4.7 %shard_map.49 = bf16[6,128,4,1024]{3,2,1,0:T(4,128)(2,1)} custom-call(bf16[128,3,32,128]{3,2,1,0:T(8,128)(2,1)S(1)} %collective-permute-done.far_ref, bf16[1024,1024]{1,0:T(8,128)(2,1)S(1)} %get-tuple-element.8.table_ref, f32[1,1024]{1,0:T(1,128)S(1)} %get-tuple-element.9.taper_ref, ...), custom_call_target="tpu_custom_call", output_to_operand_aliasing={{}: (3, {})} | custom-call | flops 6000000000 | bytes 10000000 | tf_op jit(solution)/shard_map/pallas_call | solution.py:246
Async XLA Ops:
  2.4 44.1 %copy-start = (s32[6]{0:T(128)S(1)}, s32[6]{0:T(128)}, u32[]{:S(2)}) copy-start(s32[6]{0:T(128)} %plan.1) | copy-start | bytes 76
  94.6 6.9 %collective-permute-start = (bf16[128,3,32,128]{3,2,1,0:T(8,128)(2,1)S(1)}, bf16[128,3,32,128]{3,2,1,0:T(8,128)(2,1)S(1)}, u32[]{:S(2)}, u32[]{:S(2)}) collective-permute-start(bf16[128,3,32,128]{3,2,1,0:T(8,128)(2,1)S(1)} %all_to_all.11.own_ref), channel_id=1, source_target_pairs={{0,32},{32,0},{64,96},{96,64},{1,33},{33,1},{65,97},{97,65},{2,34}... | collective-permute-start | bytes 9437192 | tf_op jit(solution)/shard_map/ppermute | solution.py:264

commit v7 on v6

--- a/solution.py
+++ b/solution.py
@@ -16,7 +16,7 @@
 SHARE = 3
 LOCAL_WIN = 8
 FINE = 4
-ROWS = 72
+TILES = 17
 GROUPS = 4
 F32 = jnp.float32
 BF16 = jnp.bfloat16
@@ -32,30 +32,24 @@
     usable = jnp.zeros((1, 128), F32)
     for w in range(LOCAL_WIN):
         for r in range(4):
-            usable = jnp.where(lane == 4 * w + r, mask_ref[r, w].astype(F32), usable)
-    block[:, 32:, :] = jnp.zeros((2, 96, 128), F32)
-    low = lax.broadcasted_iota(jnp.int32, (128, 128), 0) % 8 < 4
-
-    def split(first, second):
-        down = pltpu.roll(second, 4, 0)
-        up = pltpu.roll(first, 124, 0)
-        return jnp.where(low, first, down), jnp.where(low, up, second)
+            usable = jnp.where(lane % 32 == 4 * w + r, mask_ref[r, w].astype(F32), usable)
+    block[64:, :] = jnp.zeros((64, 128), F32)
+
+    def put(b, tile, turned):
+        for core in range(2):
+            chans = slice(32 * core + 16 * b, 32 * core + 16 * b + 16)
+            out_ref[chans, tile] = turned.reshape(16, 2, 4, 128)[:, core].astype(BF16)
 
     for b in range(2):
         lanes = slice(128 * b, 128 * b + 128)
         for part, ref in enumerate((rec_re_ref, rec_im_ref)):
             for w in range(LOCAL_WIN):
-                block[part, 4 * w : 4 * w + 4, :] = ref[w, :, lanes].astype(F32)
-        for core, tiles in enumerate(split(block[0].T * usable, block[1].T * usable)):
-            out_ref[32 * core + 16 * b : 32 * core + 16 * b + 16, 64:, :] = tiles.reshape(16, 8, 128).astype(BF16)
+                row = 32 * part + 4 * w
+                block[row : row + 4, :] = ref[w, :, lanes].astype(F32)
+        put(b, TILES - 1, block[...].T * usable)
         for part, ref in enumerate((re_ref, im_ref)):
-            for w in range(0, LOCAL_WIN, 4):
-                turned = [ref[w + k, :, lanes].astype(F32).T for k in range(4)]
-                cores = zip(split(turned[0], turned[1]), split(turned[2], turned[3]))
-                row = 32 * part + 4 * w
-                for core, pair in enumerate(cores):
-                    both = jnp.concatenate([tiles.reshape(16, 8, 128) for tiles in pair], axis=1)
-                    out_ref[32 * core + 16 * b : 32 * core + 16 * b + 16, row : row + 16, :] = both.astype(BF16)
+            for w in range(LOCAL_WIN):
+                put(b, LOCAL_WIN * part + w, ref[w, :, lanes].astype(F32).T)
 
 
 def pack(source_spectra, receiver_spectra, quality_mask):
@@ -69,28 +63,27 @@
             pl.BlockSpec((LOCAL_WIN, 4, 256), lambda b: (0, 0, b)),
             pl.BlockSpec((LOCAL_WIN, 4, 256), lambda b: (0, 0, b + 2)),
         ],
-        out_specs=pl.BlockSpec((64, ROWS, 128), lambda b: (b, 0, 0)),
-        out_shape=pltpu.VMEM((GROUPS * HOLDERS, ROWS, 128), BF16),
-        scratch_shapes=[pltpu.VMEM((2, 128, 128), F32)],
+        out_specs=pl.BlockSpec((64, TILES, 4, 128), lambda b: (b, 0, 0, 0)),
+        out_shape=pltpu.VMEM((GROUPS * HOLDERS, TILES, 4, 128), BF16),
+        scratch_shapes=[pltpu.VMEM((128, 128), F32)],
         compiler_params=params(58),
     )(quality_mask.T, source_spectra, source_spectra, receiver_spectra, receiver_spectra)
 
 
 def stack_kernel(plan, held_ref, out_ref, spread, chosen, weights, tall):
-    flat = held_ref[:, :, 64:, :].reshape(GROUPS * HOLDERS * 8, 128)
+    flat = held_ref[:, :, TILES - 1].astype(F32).reshape(GROUPS * HOLDERS * FINE, 128).astype(BF16)
     row = lax.broadcasted_iota(jnp.int32, (128, 256), 0)
     lane = lax.broadcasted_iota(jnp.int32, (128, 256), 1)
-    holder = lax.broadcasted_iota(jnp.int32, (HOLDERS, 8, 256), 0)
-    here = lax.broadcasted_iota(jnp.int32, (HOLDERS, 8, 256), 2) % 128 // 4 == holder
-    for w in range(0, LOCAL_WIN, 2):
-        place = jnp.where(row == 4 * (w + lane // 128) + lane % 4, 1.0, 0.0).astype(BF16)
-        tiled = jnp.dot(flat, place, preferred_element_type=F32).reshape(GROUPS, HOLDERS, 8, 256)
+    holder = 2 * lax.broadcasted_iota(jnp.int32, (16, 8, 256), 0) + lax.broadcasted_iota(jnp.int32, (16, 8, 256), 1) // 4
+    here = lax.broadcasted_iota(jnp.int32, (16, 8, 256), 2) % 128 // 4 == holder
+    for k in range(0, 2 * LOCAL_WIN, 2):
+        place = jnp.where(row == 4 * (k + lane // 128) + lane % 4, 1.0, 0.0).astype(BF16)
+        tiled = jnp.dot(flat, place, preferred_element_type=F32).reshape(GROUPS, 16, 8, 256)
         for group in range(GROUPS):
             two = jnp.sum(jnp.where(here, tiled[group], 0.0), axis=0)
-            for k in range(2):
-                for part in range(2):
-                    one = two[FINE * part : FINE * part + FINE, 128 * k : 128 * k + 128]
-                    spread[group, pl.ds(LOCAL_WIN * part + w + k, FINE, stride=16), :] = one
+            two = two[:FINE] + two[FINE:]
+            for j in range(2):
+                spread[group, pl.ds(k + j, FINE, stride=16), :] = two[:, 128 * j : 128 * j + 128]
     for i in range(FINE):
         real, imag = [], []
         for group in range(GROUPS):
@@ -103,7 +96,7 @@
     for step in range(0, STEPS, 2):
         for k in range(2):
             for group in range(GROUPS):
-                chosen[k, group] = held_ref[group, plan[step + k], :64, :].astype(F32)
+                chosen[k, group] = held_ref[group, plan[step + k], :16].astype(F32).reshape(64, 128)
         for i in range(FINE):
             pair = [
                 jnp.concatenate([chosen[k, group, pl.ds(i, 16, stride=FINE), :] for group in range(GROUPS)], axis=0)
@@ -259,7 +252,7 @@
 
 def shards(source_spectra, receiver_spectra, quality_mask, owner_plan):
     packed = pack(source_spectra, receiver_spectra, quality_mask)
-    held = exchange(packed).reshape(GROUPS, HOLDERS, ROWS, 128)
+    held = exchange(packed).reshape(GROUPS, HOLDERS, TILES, 4, 128)
     own = exchange(stack(owner_plan, held))
     far = lax.ppermute(own, "win", CORE_SWAP)
     out, table, taper = begin(own, LAGS // GROUPS)

time: 106 us -> 105 us (level)
  blocking collectives: 90 us -> 88.6 us
    all_to_all x2, blocking collectives: 90 us -> 88.6 us  [exchange(): return lax.all_to_all(blocks, ('win', 'chan'), 0, 0, tiled=True)]
where the time goes in v7:
time: 105 us
  blocking collectives  88.6 us (84%)
  Pallas kernels  14.8 us (14%)
  starting transfers between devices  1.14 us (1%)
    all_to_all x2, blocking collectives, exchange(): return lax.all_to_all(blocks, ('win', 'chan'), 0, 0, tiled=True)  88.6 us
    pallas_call x1, Pallas kernels, begin(): pl.pallas_call(begin_kernel, out_specs=[pl.BlockSpec(memory_space=pl.ANY)...  5.72 us
    pallas_call x1, Pallas kernels, finish(): pl.pallas_call(finish_kernel, in_specs=[vmem, vmem, vmem, pl.BlockSpec(me...  4.68 us
    pallas_call x1, Pallas kernels, stack(): pl.pallas_call(stack_kernel, in_specs=[pl.BlockSpec(memory_space=pltpu.SM...  2.24 us
    pallas_call x1, Pallas kernels, pack(): pl.pallas_call(pack_kernel, grid=(2,), in_specs=[pl.BlockSpec(memory_spac...  2.19 us
  transfers between devices with their start and end apart: 1, of which 0 were waited for; matrix products, arithmetic and copies ran while one was open for 0% of the time, Pallas kernels for 5%

profile of v7, /device:TPU:1, one launch (start us, length us, event | category | flops | bytes accessed | tf_op | source)
XLA Modules:
  0.0 104.7 jit_solution(15247565449018419362)
XLA Ops:
  0.0 2.2 %shard_map.46 = bf16[128,17,4,128]{3,2,1,0:T(4,128)(2,1)S(1)} custom-call(s32[4,8]{1,0:T(4,128)} %bitcast.5, bf16[8,128,1024]{2,1,0:T(8,128)(2,1)} %im_ref.1, bf16[8,128,1024]{2,1,0:T(8,128)(2,1)} %im_ref.1, bf16[8,4,1024]{2,1,0:T(4,128)(2,1)} %rec_im_ref.1, bf16[8,4,1024]{2,1,0:T(4,128)(2,1)} %rec_im_ref.1), custom_call_target="tpu_custom_call" | custom-call | tf_op jit(solution)/shard_map/pallas_call | solution.py:56
  2.2 0.0 copy-start
  2.2 42.4 %all_to_all.10 = bf16[128,17,4,128]{3,2,1,0:T(4,128)(2,1)S(1)} all-to-all(bf16[128,17,4,128]{3,2,1,0:T(4,128)(2,1)S(1)} %shard_map.46), channel_id=1, replica_groups=mesh['win'=4,'chan'=32] {'win','chan'}, dimensions={0} | all-to-all | bytes 4456448 | tf_op jit(solution)/shard_map/all_to_all | solution.py:250
  44.6 0.0 copy-done
  44.6 2.2 %shard_map.47 = bf16[4,32,3,32,128]{4,3,2,1,0:T(8,128)(2,1)S(1)} custom-call(s32[6]{0:T(128)S(1)} %copy-done, bf16[4,32,17,4,128]{4,3,2,1,0:T(4,128)(2,1)S(1)} %bitcast.4), custom_call_target="tpu_custom_call" | custom-call | tf_op jit(solution)/shard_map/pallas_call | solution.py:117
  46.9 46.2 %all_to_all.11.own_ref = bf16[128,3,32,128]{3,2,1,0:T(8,128)(2,1)S(1)} all-to-all(bf16[128,3,32,128]{3,2,1,0:T(8,128)(2,1)S(1)} %bitcast.3), channel_id=1, replica_groups=mesh['win'=4,'chan'=32] {'win','chan'}, dimensions={0} | all-to-all | bytes 6291456 | tf_op jit(solution)/shard_map/all_to_all | solution.py:250
  93.1 1.1 %collective-permute-start = (bf16[128,3,32,128]{3,2,1,0:T(8,128)(2,1)S(1)}, bf16[128,3,32,128]{3,2,1,0:T(8,128)(2,1)S(1)}, u32[]{:S(2)}, u32[]{:S(2)}) collective-permute-start(bf16[128,3,32,128]{3,2,1,0:T(8,128)(2,1)S(1)} %all_to_all.11.own_ref), channel_id=1, source_target_pairs={{0,32},{32,0},{64,96},{96,64},{1,33},{33,1},{65,97},{97,65},{2,34}... | collective-permute-start | bytes 9437192 | tf_op jit(solution)/shard_map/ppermute | solution.py:257
  94.2 5.7 %shard_map.48 = (bf16[6,128,4,1024]{3,2,1,0:T(4,128)(2,1)}, bf16[1024,1024]{1,0:T(8,128)(2,1)S(1)}, f32[1,1024]{1,0:T(1,128)S(1)}) custom-call(bf16[128,3,32,128]{3,2,1,0:T(8,128)(2,1)S(1)} %all_to_all.11.own_ref), custom_call_target="tpu_custom_call" | custom-call | flops 6000000000 | bytes 10000000 | tf_op jit(solution)/shard_map/pallas_call | solution.py:225
  100.0 0.0 collective-permute-done.far_ref
  100.0 4.7 %shard_map.49 = bf16[6,128,4,1024]{3,2,1,0:T(4,128)(2,1)} custom-call(bf16[128,3,32,128]{3,2,1,0:T(8,128)(2,1)S(1)} %collective-permute-done.far_ref, bf16[1024,1024]{1,0:T(8,128)(2,1)S(1)} %get-tuple-element.8.table_ref, f32[1,1024]{1,0:T(1,128)S(1)} %get-tuple-element.9.taper_ref, ...), custom_call_target="tpu_custom_call", output_to_operand_aliasing={{}: (3, {})} | custom-call | flops 6000000000 | bytes 10000000 | tf_op jit(solution)/shard_map/pallas_call | solution.py:239
Async XLA Ops:
  2.2 42.4 %copy-start = (s32[6]{0:T(128)S(1)}, s32[6]{0:T(128)}, u32[]{:S(2)}) copy-start(s32[6]{0:T(128)} %plan.1) | copy-start | bytes 76
  93.1 6.9 %collective-permute-start = (bf16[128,3,32,128]{3,2,1,0:T(8,128)(2,1)S(1)}, bf16[128,3,32,128]{3,2,1,0:T(8,128)(2,1)S(1)}, u32[]{:S(2)}, u32[]{:S(2)}) collective-permute-start(bf16[128,3,32,128]{3,2,1,0:T(8,128)(2,1)S(1)} %all_to_all.11.own_ref), channel_id=1, source_target_pairs={{0,32},{32,0},{64,96},{96,64},{1,33},{33,1},{65,97},{97,65},{2,34}... | collective-permute-start | bytes 9437192 | tf_op jit(solution)/shard_map/ppermute | solution.py:257

commit v8 on v7

--- a/solution.py
+++ b/solution.py
@@ -148,8 +148,18 @@
     index = lax.broadcasted_iota(jnp.int32, (8, count), 0)
 
     def waves(wave):
-        angle = ((wave * shift) & (2 * LAGS - 1)).astype(F32) * (math.pi / LAGS)
-        return jnp.cos(angle), jnp.sin(angle)
+        phase = (wave * shift) & (2 * LAGS - 1)
+        quadrant = (phase + 1024) >> 11
+        x = (phase - (quadrant << 11)).astype(F32) * (math.pi / LAGS)
+        y = x * x
+        cos = 1 + y * (-1 / 2 + y * (1 / 24 + y * (-1 / 720 + y * (1 / 40320 - y * (1 / 3628800)))))
+        sin = x * (1 + y * (-1 / 6 + y * (1 / 120 + y * (-1 / 5040 + y * (1 / 362880)))))
+        odd = (quadrant & 1) == 1
+        first, second = jnp.where(odd, sin, cos), jnp.where(odd, cos, sin)
+        return (
+            jnp.where(((quadrant + 1) & 2) == 2, -first, first),
+            jnp.where((quadrant & 2) == 2, -second, second),
+        )
 
     high_cos, high_sin = waves(64 * index + 64)
     mid_cos, mid_sin = waves(8 * index)

time: 105 us -> 105 us (level)
  no operation moved by 1% of the time
where the time goes in v8:
time: 105 us; the launch traced here: 104 us
  blocking collectives  88.6 us (84%)
  Pallas kernels  14.6 us (14%)
  starting transfers between devices  1.14 us (1%)
    all_to_all x2, blocking collectives, exchange(): return lax.all_to_all(blocks, ('win', 'chan'), 0, 0, tiled=True)  88.6 us
    pallas_call x1, Pallas kernels, begin(): pl.pallas_call(begin_kernel, out_specs=[pl.BlockSpec(memory_space=pl.ANY)...  5.48 us
    pallas_call x1, Pallas kernels, finish(): pl.pallas_call(finish_kernel, in_specs=[vmem, vmem, vmem, pl.BlockSpec(me...  4.68 us
    pallas_call x1, Pallas kernels, stack(): pl.pallas_call(stack_kernel, in_specs=[pl.BlockSpec(memory_space=pltpu.SM...  2.23 us
    pallas_call x1, Pallas kernels, pack(): pl.pallas_call(pack_kernel, grid=(2,), in_specs=[pl.BlockSpec(memory_spac...  2.19 us
  transfers between devices with their start and end apart: 1, of which 0 were waited for; matrix products, arithmetic and copies ran while one was open for 0% of the time, Pallas kernels for 5%

profile of v8, /device:TPU:1, one launch (start us, length us, event | category | flops | bytes accessed | tf_op | source)
XLA Modules:
  0.0 104.4 jit_solution(7361813470167448715)
XLA Ops:
  0.0 2.2 %shard_map.46 = bf16[128,17,4,128]{3,2,1,0:T(4,128)(2,1)S(1)} custom-call(s32[4,8]{1,0:T(4,128)} %bitcast.5, bf16[8,128,1024]{2,1,0:T(8,128)(2,1)} %im_ref.1, bf16[8,128,1024]{2,1,0:T(8,128)(2,1)} %im_ref.1, bf16[8,4,1024]{2,1,0:T(4,128)(2,1)} %rec_im_ref.1, bf16[8,4,1024]{2,1,0:T(4,128)(2,1)} %rec_im_ref.1), custom_call_target="tpu_custom_call" | custom-call | tf_op jit(solution)/shard_map/pallas_call | solution.py:56
  2.2 0.0 copy-start
  2.2 42.4 %all_to_all.10 = bf16[128,17,4,128]{3,2,1,0:T(4,128)(2,1)S(1)} all-to-all(bf16[128,17,4,128]{3,2,1,0:T(4,128)(2,1)S(1)} %shard_map.46), channel_id=1, replica_groups=mesh['win'=4,'chan'=32] {'win','chan'}, dimensions={0} | all-to-all | bytes 4456448 | tf_op jit(solution)/shard_map/all_to_all | solution.py:260
  44.6 0.0 copy-done
  44.6 2.2 %shard_map.47 = bf16[4,32,3,32,128]{4,3,2,1,0:T(8,128)(2,1)S(1)} custom-call(s32[6]{0:T(128)S(1)} %copy-done, bf16[4,32,17,4,128]{4,3,2,1,0:T(4,128)(2,1)S(1)} %bitcast.4), custom_call_target="tpu_custom_call" | custom-call | tf_op jit(solution)/shard_map/pallas_call | solution.py:117
  46.9 46.2 %all_to_all.11.own_ref = bf16[128,3,32,128]{3,2,1,0:T(8,128)(2,1)S(1)} all-to-all(bf16[128,3,32,128]{3,2,1,0:T(8,128)(2,1)S(1)} %bitcast.3), channel_id=1, replica_groups=mesh['win'=4,'chan'=32] {'win','chan'}, dimensions={0} | all-to-all | bytes 6291456 | tf_op jit(solution)/shard_map/all_to_all | solution.py:260
  93.1 1.1 %collective-permute-start = (bf16[128,3,32,128]{3,2,1,0:T(8,128)(2,1)S(1)}, bf16[128,3,32,128]{3,2,1,0:T(8,128)(2,1)S(1)}, u32[]{:S(2)}, u32[]{:S(2)}) collective-permute-start(bf16[128,3,32,128]{3,2,1,0:T(8,128)(2,1)S(1)} %all_to_all.11.own_ref), channel_id=1, source_target_pairs={{0,32},{32,0},{64,96},{96,64},{1,33},{33,1},{65,97},{97,65},{2,34}... | collective-permute-start | bytes 9437192 | tf_op jit(solution)/shard_map/ppermute | solution.py:267
  94.2 5.5 %shard_map.48 = (bf16[6,128,4,1024]{3,2,1,0:T(4,128)(2,1)}, bf16[1024,1024]{1,0:T(8,128)(2,1)S(1)}, f32[1,1024]{1,0:T(1,128)S(1)}) custom-call(bf16[128,3,32,128]{3,2,1,0:T(8,128)(2,1)S(1)} %all_to_all.11.own_ref), custom_call_target="tpu_custom_call" | custom-call | flops 6000000000 | bytes 10000000 | tf_op jit(solution)/shard_map/pallas_call | solution.py:235
  99.7 0.0 collective-permute-done.far_ref
  99.7 4.7 %shard_map.49 = bf16[6,128,4,1024]{3,2,1,0:T(4,128)(2,1)} custom-call(bf16[128,3,32,128]{3,2,1,0:T(8,128)(2,1)S(1)} %collective-permute-done.far_ref, bf16[1024,1024]{1,0:T(8,128)(2,1)S(1)} %get-tuple-element.8.table_ref, f32[1,1024]{1,0:T(1,128)S(1)} %get-tuple-element.9.taper_ref, ...), custom_call_target="tpu_custom_call", output_to_operand_aliasing={{}: (3, {})} | custom-call | flops 6000000000 | bytes 10000000 | tf_op jit(solution)/shard_map/pallas_call | solution.py:249
Async XLA Ops:
  2.2 42.4 %copy-start = (s32[6]{0:T(128)S(1)}, s32[6]{0:T(128)}, u32[]{:S(2)}) copy-start(s32[6]{0:T(128)} %plan.1) | copy-start | bytes 76
  93.1 6.6 %collective-permute-start = (bf16[128,3,32,128]{3,2,1,0:T(8,128)(2,1)S(1)}, bf16[128,3,32,128]{3,2,1,0:T(8,128)(2,1)S(1)}, u32[]{:S(2)}, u32[]{:S(2)}) collective-permute-start(bf16[128,3,32,128]{3,2,1,0:T(8,128)(2,1)S(1)} %all_to_all.11.own_ref), channel_id=1, source_target_pairs={{0,32},{32,0},{64,96},{96,64},{1,33},{33,1},{65,97},{97,65},{2,34}... | collective-permute-start | bytes 9437192 | tf_op jit(solution)/shard_map/ppermute | solution.py:267

commit v9 on v8

--- a/solution.py
+++ b/solution.py
@@ -188,24 +188,28 @@
     count = table_ref.shape[1]
     lhs = (even, odd)
 
+    cuts = [[0, 64, 128]] * (SHARE - 1) + [[0, 64, 96, 128]]
+
     def send(step, piece):
-        sources = pl.ds(64 * piece, 64)
+        at, end = cuts[step][piece : piece + 2]
+        sources = pl.ds(at, end - at)
         return pltpu.make_async_copy(ready.at[step, sources], out_ref.at[first + step, sources], sems.at[step, piece])
 
     arrange(held_ref, 0, even)
     for step in range(SHARE):
         block = rows(lhs[step % 2])
-        for piece in range(2):
-            here = slice(256 * piece, 256 * piece + 256)
+        for piece in range(len(cuts[step]) - 1):
+            at, end = cuts[step][piece : piece + 2]
             for n in range(0, count, 256):
                 lags = slice(n, n + 256)
-                total = jnp.dot(block[here], table_ref[:, lags], preferred_element_type=F32) * taper_ref[:, lags]
-                ready[step, 64 * piece : 64 * piece + 64, :, lags] = total.reshape(64, 4, 256).astype(BF16)
+                total = jnp.dot(block[4 * at : 4 * end], table_ref[:, lags], preferred_element_type=F32)
+                total = (total * taper_ref[:, lags]).reshape(end - at, 4, 256)
+                ready[step, at:end, :, lags] = total.astype(BF16)
             send(step, piece).start()
         if step + 1 < SHARE:
             arrange(held_ref, step + 1, lhs[1 - step % 2])
     for step in range(SHARE):
-        for piece in range(2):
+        for piece in range(len(cuts[step]) - 1):
             send(step, piece).wait()
 
 
@@ -224,7 +228,7 @@
             pltpu.VMEM((BLOCKS, 512, 128), F32),
             pltpu.VMEM((BLOCKS, 512, 128), F32),
             pltpu.VMEM((SHARE, SRC, 4, count), BF16),
-            pltpu.SemaphoreType.DMA((SHARE, 2)),
+            pltpu.SemaphoreType.DMA((SHARE, 3)),
         ],
         compiler_params=params(16),
         cost_estimate=pl.CostEstimate(flops=SHARE * 2_000_000_000, bytes_accessed=10_000_000, transcendentals=0),

time: 105 us -> 105 us (level)
  no operation moved by 1% of the time
where the time goes in v9:
time: 105 us; the launch traced here: 104 us
  blocking collectives  88.6 us (84%)
  Pallas kernels  14.7 us (14%)
  starting transfers between devices  1.14 us (1%)
    all_to_all x2, blocking collectives, exchange(): return lax.all_to_all(blocks, ('win', 'chan'), 0, 0, tiled=True)  88.6 us
    pallas_call x1, Pallas kernels, begin(): pl.pallas_call(begin_kernel, out_specs=[pl.BlockSpec(memory_space=pl.ANY)...  5.52 us
    pallas_call x1, Pallas kernels, finish(): pl.pallas_call(finish_kernel, in_specs=[vmem, vmem, vmem, pl.BlockSpec(me...  4.7 us
    pallas_call x1, Pallas kernels, stack(): pl.pallas_call(stack_kernel, in_specs=[pl.BlockSpec(memory_space=pltpu.SM...  2.24 us
    pallas_call x1, Pallas kernels, pack(): pl.pallas_call(pack_kernel, grid=(2,), in_specs=[pl.BlockSpec(memory_spac...  2.19 us
  transfers between devices with their start and end apart: 1, of which 0 were waited for; matrix products, arithmetic and copies ran while one was open for 0% of the time, Pallas kernels for 5%

profile of v9, /device:TPU:1, one launch (start us, length us, event | category | flops | bytes accessed | tf_op | source)
XLA Modules:
  0.0 104.5 jit_solution(4696162259153045599)
XLA Ops:
  0.0 2.2 %shard_map.46 = bf16[128,17,4,128]{3,2,1,0:T(4,128)(2,1)S(1)} custom-call(s32[4,8]{1,0:T(4,128)} %bitcast.5, bf16[8,128,1024]{2,1,0:T(8,128)(2,1)} %im_ref.1, bf16[8,128,1024]{2,1,0:T(8,128)(2,1)} %im_ref.1, bf16[8,4,1024]{2,1,0:T(4,128)(2,1)} %rec_im_ref.1, bf16[8,4,1024]{2,1,0:T(4,128)(2,1)} %rec_im_ref.1), custom_call_target="tpu_custom_call" | custom-call | tf_op jit(solution)/shard_map/pallas_call | solution.py:56
  2.2 0.0 copy-start
  2.2 42.4 %all_to_all.10 = bf16[128,17,4,128]{3,2,1,0:T(4,128)(2,1)S(1)} all-to-all(bf16[128,17,4,128]{3,2,1,0:T(4,128)(2,1)S(1)} %shard_map.46), channel_id=1, replica_groups=mesh['win'=4,'chan'=32] {'win','chan'}, dimensions={0} | all-to-all | bytes 4456448 | tf_op jit(solution)/shard_map/all_to_all | solution.py:264
  44.6 0.0 copy-done
  44.6 2.2 %shard_map.47 = bf16[4,32,3,32,128]{4,3,2,1,0:T(8,128)(2,1)S(1)} custom-call(s32[6]{0:T(128)S(1)} %copy-done, bf16[4,32,17,4,128]{4,3,2,1,0:T(4,128)(2,1)S(1)} %bitcast.4), custom_call_target="tpu_custom_call" | custom-call | tf_op jit(solution)/shard_map/pallas_call | solution.py:117
  46.9 46.2 %all_to_all.11.own_ref = bf16[128,3,32,128]{3,2,1,0:T(8,128)(2,1)S(1)} all-to-all(bf16[128,3,32,128]{3,2,1,0:T(8,128)(2,1)S(1)} %bitcast.3), channel_id=1, replica_groups=mesh['win'=4,'chan'=32] {'win','chan'}, dimensions={0} | all-to-all | bytes 6291456 | tf_op jit(solution)/shard_map/all_to_all | solution.py:264
  93.1 1.1 %collective-permute-start = (bf16[128,3,32,128]{3,2,1,0:T(8,128)(2,1)S(1)}, bf16[128,3,32,128]{3,2,1,0:T(8,128)(2,1)S(1)}, u32[]{:S(2)}, u32[]{:S(2)}) collective-permute-start(bf16[128,3,32,128]{3,2,1,0:T(8,128)(2,1)S(1)} %all_to_all.11.own_ref), channel_id=1, source_target_pairs={{0,32},{32,0},{64,96},{96,64},{1,33},{33,1},{65,97},{97,65},{2,34}... | collective-permute-start | bytes 9437192 | tf_op jit(solution)/shard_map/ppermute | solution.py:271
  94.2 5.5 %shard_map.48 = (bf16[6,128,4,1024]{3,2,1,0:T(4,128)(2,1)}, bf16[1024,1024]{1,0:T(8,128)(2,1)S(1)}, f32[1,1024]{1,0:T(1,128)S(1)}) custom-call(bf16[128,3,32,128]{3,2,1,0:T(8,128)(2,1)S(1)} %all_to_all.11.own_ref), custom_call_target="tpu_custom_call" | custom-call | flops 6000000000 | bytes 10000000 | tf_op jit(solution)/shard_map/pallas_call | solution.py:239
  99.8 0.0 collective-permute-done.far_ref
  99.8 4.7 %shard_map.49 = bf16[6,128,4,1024]{3,2,1,0:T(4,128)(2,1)} custom-call(bf16[128,3,32,128]{3,2,1,0:T(8,128)(2,1)S(1)} %collective-permute-done.far_ref, bf16[1024,1024]{1,0:T(8,128)(2,1)S(1)} %get-tuple-element.8.table_ref, f32[1,1024]{1,0:T(1,128)S(1)} %get-tuple-element.9.taper_ref, ...), custom_call_target="tpu_custom_call", output_to_operand_aliasing={{}: (3, {})} | custom-call | flops 6000000000 | bytes 10000000 | tf_op jit(solution)/shard_map/pallas_call | solution.py:253
Async XLA Ops:
  2.2 42.4 %copy-start = (s32[6]{0:T(128)S(1)}, s32[6]{0:T(128)}, u32[]{:S(2)}) copy-start(s32[6]{0:T(128)} %plan.1) | copy-start | bytes 76
  93.1 6.7 %collective-permute-start = (bf16[128,3,32,128]{3,2,1,0:T(8,128)(2,1)S(1)}, bf16[128,3,32,128]{3,2,1,0:T(8,128)(2,1)S(1)}, u32[]{:S(2)}, u32[]{:S(2)}) collective-permute-start(bf16[128,3,32,128]{3,2,1,0:T(8,128)(2,1)S(1)} %all_to_all.11.own_ref), channel_id=1, source_target_pairs={{0,32},{32,0},{64,96},{96,64},{1,33},{33,1},{65,97},{97,65},{2,34}... | collective-permute-start | bytes 9437192 | tf_op jit(solution)/shard_map/ppermute | solution.py:271
